TPU v7x, 32 devices: a whole 2x2x4 slice. The times are simulated.
32 devices in a mesh: rep: 2 (over x), tp: 8 (over z, y), dp: 2 (over core).
Axes of the slice: x: 2, y: 2, z: 4, core: 2. Of those that a mesh axis runs over, the one named last changes fastest.
Arguments:
- tokens: bfloat16 [1024, 4096], P(('rep', 'dp'), 'tp'), parts along dimension 0, may hold values from -6 to 6
- gate_weight: bfloat16 [4096, 14336], P('dp', 'tp'), may hold values from -0.125 to 0.125
- up_weight: bfloat16 [4096, 14336], P('dp', 'tp'), may hold values from -0.125 to 0.125
- down_weight: bfloat16 [14336, 4096], P('tp', 'dp'), may hold values from -0.0625 to 0.0625
- out_grad: bfloat16 [1024, 4096], P(('rep', 'dp'), 'tp'), parts along dimension 0, may hold values from -6 to 6
Outputs:
- output: bfloat16 [1024, 4096], P(('rep', 'dp'), 'tp'), parts along dimension 0
- input_grad: bfloat16 [1024, 4096], P(('rep', 'dp'), 'tp'), parts along dimension 0
- gate_wgrad: bfloat16 [8192, 14336], P(('rep', 'dp'), 'tp'), parts along dimension 0
- up_wgrad: bfloat16 [8192, 14336], P(('rep', 'dp'), 'tp'), parts along dimension 0
- down_wgrad: bfloat16 [14336, 8192], P('tp', ('rep', 'dp')), parts along dimension 1
There are 2 independent parts, one for each index of `rep`. A program takes and returns all parts, laid end to end along the dimension named above; an argument that names none is the same for every part. Nothing has to cross between parts.
All inputs are finite; a program needn't handle non-finite values.
Results may differ from a plain program's by a relative error of at most 0.013.
Values may be sent and summed in bfloat16 or wider, within the bound.
No kernel may reach another device: no remote copies, remote signals or barrier semaphores. Data moves between devices by JAX's collectives and lax.ppermute only.
A program may use at most 256 MiB of HBM per device.

v0:
```python
import jax
import jax.numpy as jnp
from jax import lax
from jax.sharding import PartitionSpec as P


def contract_last(left, right):
    return lax.dot_general(
        left, right, (((1,), (1,)), ((), ())), preferred_element_type=jnp.float32
    )


def contract_first(left, right):
    return lax.dot_general(
        left, right, (((0,), (0,)), ((), ())), preferred_element_type=jnp.float32
    )


def local_grads(hidden_grad, gate_value, up_value):
    sigmoid_gate = jax.nn.sigmoid(gate_value)
    activated = gate_value * sigmoid_gate
    gate_grad = (
        hidden_grad * up_value * sigmoid_gate * (1.0 + gate_value * (1.0 - sigmoid_gate))
    ).astype(jnp.bfloat16)
    up_grad = (hidden_grad * activated).astype(jnp.bfloat16)
    return (gate_grad, up_grad)


def hidden_of(gate_value, up_value):
    return (jax.nn.silu(gate_value) * up_value).astype(jnp.bfloat16)


def body(tokens, gate_weight, up_weight, down_weight, out_grad):
    tokens_all, grad_all = (
        lax.all_gather(tokens, "tp", axis=1, tiled=True),
        lax.all_gather(out_grad, "tp", axis=1, tiled=True),
    )
    gate_full, up_full, down_full = (
        lax.all_gather(gate_weight, "dp", axis=0, tiled=True),
        lax.all_gather(up_weight, "dp", axis=0, tiled=True),
        lax.all_gather(down_weight, "dp", axis=1, tiled=True),
    )
    gate_value = jnp.dot(tokens_all, gate_full, preferred_element_type=jnp.float32)
    up_value = jnp.dot(tokens_all, up_full, preferred_element_type=jnp.float32)
    hidden = hidden_of(gate_value, up_value)
    out_terms = jnp.dot(hidden, down_full, preferred_element_type=jnp.float32)
    hidden_grad = contract_last(grad_all, down_full)
    gate_grad, up_grad = local_grads(hidden_grad, gate_value, up_value)
    in_terms = contract_last(gate_grad, gate_full) + contract_last(up_grad, up_full)
    gate_sum, up_sum, down_sum = (
        lax.psum_scatter(
            contract_first(tokens_all, gate_grad).astype(jnp.bfloat16),
            "dp",
            scatter_dimension=0,
            tiled=True,
        ).astype(jnp.float32),
        lax.psum_scatter(
            contract_first(tokens_all, up_grad).astype(jnp.bfloat16),
            "dp",
            scatter_dimension=0,
            tiled=True,
        ).astype(jnp.float32),
        lax.psum_scatter(
            contract_first(hidden, grad_all).astype(jnp.bfloat16),
            "dp",
            scatter_dimension=1,
            tiled=True,
        ).astype(jnp.float32),
    )
    gate_wgrad = gate_sum.astype(jnp.bfloat16)
    up_wgrad = up_sum.astype(jnp.bfloat16)
    down_wgrad = down_sum.astype(jnp.bfloat16)
    output = lax.psum_scatter(out_terms.astype(jnp.bfloat16), "tp", scatter_dimension=1, tiled=True)
    input_grad = lax.psum_scatter(
        in_terms.astype(jnp.bfloat16), "tp", scatter_dimension=1, tiled=True
    )
    return (output, input_grad, gate_wgrad, up_wgrad, down_wgrad)


def solution(mesh):
    in_specs = (
        P(("rep", "dp"), "tp"),
        P("dp", "tp"),
        P("dp", "tp"),
        P("tp", "dp"),
        P(("rep", "dp"), "tp"),
    )
    out_specs = (
        P(("rep", "dp"), "tp"),
        P(("rep", "dp"), "tp"),
        P(("rep", "dp"), "tp"),
        P(("rep", "dp"), "tp"),
        P("tp", ("rep", "dp")),
    )
    return jax.shard_map(body, mesh=mesh, in_specs=in_specs, out_specs=out_specs, check_vma=False)
```

profile of v0, /device:TPU:0, one launch (start us, length us, event | category | flops | bytes accessed | tf_op | source)
XLA Modules:
  0.0 452.3 jit_solution(9278657264522810182)
XLA Ops:
  7.2 0.7 all-gather.6.cloned.1.call-update
  7.9 0.7 all-gather.10.cloned.1.call-update
  8.7 0.7 all-gather.8.cloned.1.call-update
  10.6 53.3 %all-gather.6.cloned.1.call-done = bf16[256,4096]{1,0:T(8,128)(2,1)} async-done(((bf16[256,512]{1,0:T(8,128)(2,1)}), bf16[256,4096]{1,0:T(8,128)(2,1)}) %all-gather.6.cloned.1.call-update) | async-done | bytes 2097168 | tf_op jit(solution)/shard_map/all_gather | solution.py:35
  63.8 26.8 %all-gather.10.cloned.1.call-done = bf16[4096,1792]{1,0:T(8,128)(2,1)} async-done(((bf16[2048,1792]{1,0:T(8,128)(2,1)}), bf16[4096,1792]{1,0:T(8,128)(2,1)}) %all-gather.10.cloned.1.call-update) | async-done | bytes 14680080 | tf_op jit(solution)/shard_map/all_gather | solution.py:40
  90.7 11.0 %fusion.5 = f32[256,1792]{1,0:T(8,128)} fusion(bf16[256,4096]{1,0:T(8,128)(2,1)} %all-gather.6.cloned.1.call-done, bf16[4096,1792]{1,0:T(8,128)(2,1)} %all-gather.10.cloned.1.call-done), kind=kOutput, calls=%fused_computation.14 | convolution fusion | flops 3758096384 | bytes 18612224 | tf_op jit(solution)/shard_map/dot_general | solution.py:44
  101.6 18.8 %all-gather.8.cloned.1.call-done = bf16[4096,1792]{1,0:T(8,128)(2,1)} async-done(((bf16[2048,1792]{1,0:T(8,128)(2,1)}), bf16[4096,1792]{1,0:T(8,128)(2,1)}) %all-gather.8.cloned.1.call-update) | async-done | bytes 14680080 | tf_op jit(solution)/shard_map/all_gather | solution.py:39
  120.5 8.5 %fusion.4 = f32[256,1792]{1,0:T(8,128)} fusion(bf16[256,4096]{1,0:T(8,128)(2,1)S(1)} %copy-done, bf16[4096,1792]{1,0:T(8,128)(2,1)} %all-gather.8.cloned.1.call-done), kind=kOutput, calls=%fused_computation.13 | convolution fusion | flops 3758096384 | bytes 18612224 | tf_op jit(solution)/shard_map/dot_general | solution.py:43
  128.9 45.7 %all-gather.14.cloned.1.call-done = bf16[256,4096]{1,0:T(8,128)(2,1)} async-done(((bf16[256,512]{1,0:T(8,128)(2,1)}), bf16[256,4096]{1,0:T(8,128)(2,1)}) %all-gather.14.cloned.1.call-update) | async-done | bytes 2097168 | tf_op jit(solution)/shard_map/all_gather | solution.py:36
  174.6 26.7 %all-gather.12.cloned.1.call-done = bf16[1792,4096]{1,0:T(8,128)(2,1)} async-done(((bf16[1792,2048]{1,0:T(8,128)(2,1)}), bf16[1792,4096]{1,0:T(8,128)(2,1)}) %all-gather.12.cloned.1.call-update) | async-done | bytes 14680080 | tf_op jit(solution)/shard_map/all_gather | solution.py:41
  201.3 12.6 %multiply_convert_fusion = (bf16[256,1792]{1,0:T(8,128)(2,1)}, bf16[256,1792]{1,0:T(8,128)(2,1)}, bf16[256,1792]{1,0:T(8,128)(2,1)S(1)}) fusion(f32[256,1792]{1,0:T(8,128)} %fusion.4, f32[256,1792]{1,0:T(8,128)} %fusion.5, bf16[256,4096]{1,0:T(8,128)(2,1)} %all-gather.14.cloned.1.call-done, bf16[1792,4096]{1,0:T(8,128)(2,1)} %all-gather.12.cloned.1.call-done), kind=kOutput, calls=%fused_computation.8 | convolution fusion | flops 3764977664 | bytes 23199744 | tf_op jit(solution)/shard_map/dot_general | solution.py:8
  213.9 8.5 %fusion.1 = bf16[4096,1792]{0,1:T(8,128)(2,1)} fusion(bf16[256,1792]{1,0:T(8,128)(2,1)} %get-tuple-element.10, bf16[256,4096]{1,0:T(8,128)(2,1)S(1)} %copy-done), kind=kOutput, calls=%fused_computation.4 | convolution fusion | flops 3765436416 | bytes 17694720 | tf_op jit(solution)/shard_map/dot_general | solution.py:14
  222.6 9.3 %fusion = bf16[4096,1792]{0,1:T(8,128)(2,1)} fusion(bf16[256,1792]{1,0:T(8,128)(2,1)} %get-tuple-element.11, bf16[256,4096]{1,0:T(8,128)(2,1)S(1)} %copy-done), kind=kOutput, calls=%fused_computation.3 | convolution fusion | flops 3765436416 | bytes 17694720 | tf_op jit(solution)/shard_map/dot_general | solution.py:14
  232.0 1.4 copy-done.3
  233.4 19.4 %fusion.6 = f32[256,4096]{1,0:T(8,128)} fusion(bf16[256,1792]{1,0:T(8,128)(2,1)S(1)} %copy-done.3, bf16[4096,1792]{1,0:T(8,128)(2,1)} %all-gather.8.cloned.1.call-done), kind=kOutput, calls=%fused_computation.15 | convolution fusion | flops 3758096384 | bytes 19791872 | tf_op jit(solution)/shard_map/dot_general | solution.py:8
  252.7 17.7 %fusion.2 = bf16[256,4096]{1,0:T(8,128)(2,1)} fusion(f32[256,4096]{1,0:T(8,128)} %fusion.6, bf16[256,1792]{1,0:T(8,128)(2,1)S(1)} %copy-done.2, bf16[4096,1792]{1,0:T(8,128)(2,1)} %all-gather.10.cloned.1.call-done), kind=kOutput, calls=%fused_computation.7 | convolution fusion | flops 3760193536 | bytes 21889024 | tf_op jit(solution)/shard_map/dot_general | solution.py:8
  270.5 11.3 %convolution_convert_fusion.3 = bf16[256,4096]{1,0:T(8,128)(2,1)} fusion(bf16[256,1792]{1,0:T(8,128)(2,1)S(1)} %get-tuple-element.12, bf16[1792,4096]{1,0:T(8,128)(2,1)} %all-gather.12.cloned.1.call-done), kind=kOutput, calls=%fused_computation.6 | convolution fusion | flops 3759144960 | bytes 17694720 | tf_op jit(solution)/shard_map/dot_general | solution.py:46
  281.9 1.5 copy-done.1
  283.5 7.3 %convolution_convert_fusion = bf16[1792,4096]{1,0:T(8,128)(2,1)} fusion(bf16[256,1792]{1,0:T(8,128)(2,1)S(1)} %get-tuple-element.12, bf16[256,4096]{1,0:T(8,128)(2,1)S(1)} %copy-done.1), kind=kOutput, calls=%fused_computation | convolution fusion | flops 3765436416 | bytes 17694720 | tf_op jit(solution)/shard_map/dot_general | solution.py:14
  290.9 10.0 %copy.11 = bf16[2048,1792]{1,0:T(8,128)(2,1)} copy(bf16[2048,1792]{0,1:T(8,128)(2,1)} %reduce-scatter.12.cloned.1.call-done) | data formatting | bytes 14680064
  300.8 10.0 %copy.10 = bf16[2048,1792]{1,0:T(8,128)(2,1)} copy(bf16[2048,1792]{0,1:T(8,128)(2,1)} %reduce-scatter.10.cloned.1.call-done) | data formatting | bytes 14680064
  310.8 37.8 %reduce-scatter.8.cloned.1.call-done = bf16[256,512]{1,0:T(8,128)(2,1)} async-done(((bf16[256,4096]{1,0:T(8,128)(2,1)}), bf16[256,512]{1,0:T(8,128)(2,1)}) %reduce-scatter.8.cloned.1.call-update) | async-done | bytes 262160 | tf_op jit(solution)/shard_map/reduce_scatter | solution.py:74
  348.6 71.2 %reduce-scatter.6.cloned.1.call-done = bf16[256,512]{1,0:T(8,128)(2,1)} async-done(((bf16[256,4096]{1,0:T(8,128)(2,1)}), bf16[256,512]{1,0:T(8,128)(2,1)}) %reduce-scatter.6.cloned.1.call-update) | async-done | bytes 262160 | tf_op jit(solution)/shard_map/reduce_scatter | solution.py:73
  419.7 25.8 %reduce-scatter.14.cloned.1.call-done = bf16[1792,2048]{1,0:T(8,128)(2,1)} async-done(((bf16[1792,4096]{1,0:T(8,128)(2,1)}), bf16[1792,2048]{1,0:T(8,128)(2,1)}) %reduce-scatter.14.cloned.1.call-update) | async-done | bytes 7340048 | tf_op jit(solution)/shard_map/reduce_scatter | solution.py:63
  (25 shorter events, 1.7 us)
Async XLA Ops:
  7.2 56.7 %all-gather.6.cloned.1.call-start = ((), (), s32[]{:S(2)}) async-start(), calls=%async_computation.5 | async-start | bytes 2359296 | tf_op jit(solution)/shard_map/all_gather | solution.py:35
  7.9 82.8 %all-gather.10.cloned.1.call-start = ((), (), s32[]{:S(2)}) async-start(), calls=%async_computation.7 | async-start | bytes 22020096 | tf_op jit(solution)/shard_map/all_gather | solution.py:40
  8.6 111.8 %all-gather.8.cloned.1.call-start = ((), (), s32[]{:S(2)}) async-start(), calls=%async_computation.6 | async-start | bytes 22020096 | tf_op jit(solution)/shard_map/all_gather | solution.py:39
  9.4 165.3 %all-gather.14.cloned.1.call-start = ((), (), s32[]{:S(2)}) async-start(), calls=%async_computation.10 | async-start | bytes 2359296 | tf_op jit(solution)/shard_map/all_gather | solution.py:36
  10.0 191.3 %all-gather.12.cloned.1.call-start = ((), (), s32[]{:S(2)}) async-start(), calls=%async_computation.8 | async-start | bytes 22020096 | tf_op jit(solution)/shard_map/all_gather | solution.py:41
  10.5 280.3 %reduce-scatter.12.cloned.1.call-start = ((), (), s32[]{:S(2)}) async-start(), calls=%async_computation.13 | async-start | bytes 22020096 | tf_op jit(solution)/shard_map/reduce_scatter | solution.py:57
  63.8 56.6 %copy-start = (bf16[256,4096]{1,0:T(8,128)(2,1)S(1)}, bf16[256,4096]{1,0:T(8,128)(2,1)}, u32[]{:S(2)}) copy-start(bf16[256,4096]{1,0:T(8,128)(2,1)} %all-gather.6.cloned.1.call-done) | copy-start | bytes 6291460
  222.4 78.4 %reduce-scatter.10.cloned.1.call-start = ((), (), s32[]{:S(2)}) async-start(), calls=%async_computation.12 | async-start | bytes 22020096 | tf_op jit(solution)/shard_map/reduce_scatter | solution.py:51
  231.9 1.5 copy-start.3
  231.9 20.8 %copy-start.2 = (bf16[256,1792]{1,0:T(8,128)(2,1)S(1)}, bf16[256,1792]{1,0:T(8,128)(2,1)}, u32[]{:S(2)}) copy-start(bf16[256,1792]{1,0:T(8,128)(2,1)} %get-tuple-element.10) | copy-start | bytes 2752516
  232.0 116.6 %reduce-scatter.8.cloned.1.call-start = ((), (), s32[]{:S(2)}) async-start(), calls=%async_computation.11 | async-start | bytes 2359296 | tf_op jit(solution)/shard_map/reduce_scatter | solution.py:74
  270.5 149.3 %reduce-scatter.6.cloned.1.call-start = ((), (), s32[]{:S(2)}) async-start(), calls=%async_computation.9 | async-start | bytes 2359296 | tf_op jit(solution)/shard_map/reduce_scatter | solution.py:73
  281.9 1.6 copy-start.1
  281.9 163.6 %reduce-scatter.14.cloned.1.call-start = ((), (), s32[]{:S(2)}) async-start(), calls=%async_computation.14 | async-start | bytes 22020096 | tf_op jit(solution)/shard_map/reduce_scatter | solution.py:63
Sparse Core Ops, SparseCore 0:
  10.0 53.7 all-gather.5
  65.4 25.2 all-gather.9
  92.2 28.1 all-gather.7
  122.4 52.2 all-gather.13
  176.0 25.2 all-gather.11
  222.5 25.1 reduce-scatter.11
  250.1 25.1 reduce-scatter.9
  279.4 69.1 reduce-scatter.7
  352.7 67.0 reduce-scatter.5
  422.5 22.9 reduce-scatter.13
where the time goes:
time: 453 us; the launch traced here: 452 us
  waiting for transfers between devices  309 us (68%)
  matrix products  106 us (23%)
  local copies, waits for them, and re-layouts  22.8 us (5%)
  between operations  14.2 us (3%)
    reduce_scatter x1, waiting for transfers between devices, body(): lax.psum_scatter(out_terms.astype(jnp.bfloat16), 'tp', scatter_dimension=...  71.2 us
    all_gather x1, waiting for transfers between devices, body(): lax.all_gather(tokens, 'tp', axis=1, tiled=True)  53.3 us
    dot_general x3, matrix products, contract_last(): lax.dot_general(left, right, (((1,), (1,)), ((), ())), preferred_element_...  49.7 us
    all_gather x1, waiting for transfers between devices, body(): lax.all_gather(out_grad, 'tp', axis=1, tiled=True)  45.7 us
    reduce_scatter x1, waiting for transfers between devices, body(): lax.psum_scatter(in_terms.astype(jnp.bfloat16), 'tp', scatter_dimension=1...  37.8 us
    all_gather x1, waiting for transfers between devices, body(): lax.all_gather(up_weight, 'dp', axis=0, tiled=True)  26.8 us
    all_gather x1, waiting for transfers between devices, body(): lax.all_gather(down_weight, 'dp', axis=1, tiled=True)  26.7 us
    reduce_scatter x1, waiting for transfers between devices, body(): lax.psum_scatter(contract_first(hidden, grad_all).astype(jnp.bfloat16), '...  25.8 us
  transfers between devices with their start and end apart: 10, of which 8 were waited for; matrix products, arithmetic and copies ran while one was open for 23% of the time, Pallas kernels for 0%

commit v1 on v0

v1 whole, which is shorter than its diff:
```python
import jax
import jax.numpy as jnp
from jax import lax
from jax.sharding import PartitionSpec as P

BF16 = jnp.bfloat16
F32 = jnp.float32


def ring_at(position, n):
    position = lax.rem(position + 2 * n, n)
    return jnp.where(position < n // 2, 2 * position, 2 * (n - 1 - position) + 1)


def place_of(index, n):
    return jnp.where(lax.rem(index, 2) == 0, index // 2, n - 1 - index // 2)


def hops(n):
    order = list(range(0, n, 2)) + list(range(n - 1, 0, -2))
    up = [(order[i], order[(i + 1) % n]) for i in range(n)]
    return up, [(b, a) for a, b in up]


def swap_cores(value):
    return lax.ppermute(value, "dp", [(0, 1), (1, 0)])


def ring_gather(own, n):
    up, down = hops(n)
    rows = own.shape[0] // 2
    blocks = {0: own}
    a = b = own
    for step in range(1, n // 2):
        a = lax.ppermute(a, "tp", up)
        b = lax.ppermute(b, "tp", down)
        blocks[step], blocks[-step] = a, b
    a = lax.ppermute(a[:rows], "tp", up)
    b = lax.ppermute(b[rows:], "tp", down)
    blocks[n // 2] = jnp.concatenate([a, b], 0)
    return blocks


def place(blocks, n):
    rows, width = blocks[0].shape
    spot = place_of(lax.axis_index("tp"), n)
    whole = jnp.zeros((rows, n * width), blocks[0].dtype)
    for distance, block in blocks.items():
        column = ring_at(spot - distance, n) * width
        whole = lax.dynamic_update_slice(whole, block, (0, column))
    return whole


def to_feature_half(whole):
    half = whole.shape[1] // 2
    core = lax.axis_index("dp")
    keep = lax.dynamic_slice_in_dim(whole, core * half, half, 1)
    send = lax.dynamic_slice_in_dim(whole, (1 - core) * half, half, 1)
    return jnp.concatenate([keep, swap_cores(send)], 0)


def sum_cores(partial):
    rows = partial.shape[0] // 2
    return partial[:rows] + swap_cores(partial[rows:].astype(BF16)).astype(F32)


def with_other_rows(own):
    return jnp.concatenate([own, swap_cores(own)], 0)


def to_token_rows(partial):
    rows, half = partial.shape[0] // 2, partial.shape[1]
    core = lax.axis_index("dp")
    got = swap_cores(partial[rows:])
    whole = jnp.zeros((rows, 2 * half), partial.dtype)
    whole = lax.dynamic_update_slice(whole, partial[:rows], (0, core * half))
    return lax.dynamic_update_slice(whole, got, (0, (1 - core) * half))


def ring_scatter(terms, n):
    up, down = hops(n)
    rows, width = terms.shape[0], terms.shape[1] // n
    cut = rows // 2
    spot = place_of(lax.axis_index("tp"), n)

    def term(distance):
        column = ring_at(spot + distance, n) * width
        return lax.dynamic_slice(terms, (0, column), (rows, width))

    far = term(n // 2)
    a = lax.ppermute(far[:cut], "tp", up)
    b = lax.ppermute(far[cut:], "tp", down)
    for distance in range(n // 2 - 1, 0, -1):
        ahead, behind = term(distance), term(-distance)
        if a.shape[0] == cut:
            a = jnp.concatenate([ahead[:cut] + a, ahead[cut:]], 0)
            b = jnp.concatenate([behind[:cut], behind[cut:] + b], 0)
        else:
            a, b = ahead + a, behind + b
        a = lax.ppermute(a, "tp", up)
        b = lax.ppermute(b, "tp", down)
    return (term(0).astype(F32) + a.astype(F32) + b.astype(F32)).astype(BF16)


def dot(left, right, left_dim, right_dim):
    return lax.dot_general(left, right, (((left_dim,), (right_dim,)), ((), ())), preferred_element_type=F32)


def body(n, tokens, gate_weight, up_weight, down_weight, out_grad):
    tokens_half = to_feature_half(place(ring_gather(tokens, n), n))
    grad_half = to_feature_half(place(ring_gather(out_grad, n), n))

    gate_value = sum_cores(dot(tokens_half, gate_weight, 1, 0))
    up_value = sum_cores(dot(tokens_half, up_weight, 1, 0))
    sigmoid_gate = jax.nn.sigmoid(gate_value)
    activated = gate_value * sigmoid_gate
    hidden = with_other_rows((activated * up_value).astype(BF16))
    output = ring_scatter(to_token_rows(dot(hidden, down_weight, 1, 0).astype(BF16)), n)

    hidden_grad = sum_cores(dot(grad_half, down_weight, 1, 1))
    gate_grad = with_other_rows(
        (hidden_grad * up_value * sigmoid_gate * (1.0 + gate_value * (1.0 - sigmoid_gate))).astype(BF16)
    )
    up_grad = with_other_rows((hidden_grad * activated).astype(BF16))
    in_terms = dot(gate_grad, gate_weight, 1, 1) + dot(up_grad, up_weight, 1, 1)
    input_grad = ring_scatter(to_token_rows(in_terms.astype(BF16)), n)

    gate_wgrad = dot(tokens_half, gate_grad, 0, 0).astype(BF16)
    up_wgrad = dot(tokens_half, up_grad, 0, 0).astype(BF16)
    down_wgrad = dot(hidden, grad_half, 0, 0).astype(BF16)
    return output, input_grad, gate_wgrad, up_wgrad, down_wgrad


def solution(mesh):
    n = mesh.shape["tp"]
    rows = P(("rep", "dp"), "tp")
    in_specs = (rows, P("dp", "tp"), P("dp", "tp"), P("tp", "dp"), rows)
    out_specs = (rows, rows, rows, rows, P("tp", ("rep", "dp")))

    def call(*args):
        return body(n, *args)

    return jax.shard_map(call, mesh=mesh, in_specs=in_specs, out_specs=out_specs, check_vma=False)
```

time: 453 us -> 154 us (0.34)
  waiting for transfers between devices: 309 us -> 43.3 us
  matrix products: 106 us -> 51.7 us
  starting transfers between devices: 0.58 us -> 37.5 us
  between operations: 14.2 us -> 1.24 us
  local copies, waits for them, and re-layouts: 22.8 us -> 11.3 us
  other arithmetic: 0 us -> 9 us
    all_gather x5 -> x0, waiting for transfers between devices: 171 us -> none  [the longest x1 53.3 us: body(): lax.all_gather(tokens, 'tp', axis=1, tiled=True)]
    reduce_scatter x5 -> x0, waiting for transfers between devices: 135 us -> none  [the longest x1 71.2 us: body(): lax.psum_scatter(out_terms.astype(jnp.bfloat16), 'tp', scatter_dimension=...]
    dot_general x9, matrix products: 106 us -> 51.7 us  [dot(): lax.dot_general(left, right, (((left_dim,), (right_dim,)), ((), ())), pre...]
    ppermute x0 -> x42, waiting for transfers between devices: none -> 43.3 us  [the longest x6 21.4 us: ring_gather(): b = lax.ppermute(b, 'tp', down)]
    ppermute x0 -> x42, starting transfers between devices: none -> 37.5 us  [the longest x6 12.9 us: ring_gather(): b = lax.ppermute(b, 'tp', down)]
    unnamed x10 -> x52, local copies, waits for them, and re-layouts: 22.8 us -> 0.54 us
    add x0 -> x8, other arithmetic: none -> 4.96 us  [the longest x6 3.7 us: ring_scatter(): a, b = (ahead + a, behind + b)]
  transfers between devices with their start and end apart: 10 -> 42, of which waited for: 8 -> 17; matrix products, arithmetic and copies ran while one was open for 23% -> 45% of each run, Pallas kernels for 0% -> 0%
where the time goes in v1:
time: 154 us
  matrix products  51.7 us (34%)
  waiting for transfers between devices  43.3 us (28%)
  starting transfers between devices  37.5 us (24%)
  local copies, waits for them, and re-layouts  11.3 us (7%)
  other arithmetic  9 us (6%)
    dot_general x9, matrix products, dot(): lax.dot_general(left, right, (((left_dim,), (right_dim,)), ((), ())), pre...  51.7 us
    ppermute x6, waiting for transfers between devices, ring_gather(): b = lax.ppermute(b, 'tp', down)  21.4 us
    ppermute x6, starting transfers between devices, ring_gather(): b = lax.ppermute(b, 'tp', down)  12.9 us
    ppermute x6, waiting for transfers between devices, ring_scatter(): a = lax.ppermute(a, 'tp', up)  10.8 us
    ppermute x6, starting transfers between devices, ring_scatter(): b = lax.ppermute(b, 'tp', down)  8.74 us
    ppermute x10, waiting for transfers between devices, swap_cores(): return lax.ppermute(value, 'dp', [(0, 1), (1, 0)])  6.01 us
    ppermute x2, starting transfers between devices, ring_gather(): b = lax.ppermute(b[rows:], 'tp', down)  4.11 us
    ppermute x2, starting transfers between devices, ring_scatter(): b = lax.ppermute(far[cut:], 'tp', down)  3.89 us
  transfers between devices with their start and end apart: 42, of which 17 were waited for; matrix products, arithmetic and copies ran while one was open for 45% of the time, Pallas kernels for 0%

profile of v1, /device:TPU:0, one launch (start us, length us, event | category | flops | bytes accessed | tf_op | source)
XLA Modules:
  0.0 154.0 jit_solution(16343232433172627584)
XLA Ops:
  0.6 3.0 %collective-permute-start.1 = (bf16[256,512]{1,0:T(8,128)(2,1)}, bf16[256,512]{1,0:T(8,128)(2,1)S(1)}, u32[]{:S(2)}, u32[]{:S(2)}) collective-permute-start(bf16[256,512]{1,0:T(8,128)(2,1)} %param.5), channel_id=1, source_target_pairs={{4,0},{8,4},{12,8},{14,12},{10,14},{6,10},{2,6},{0,2},{5,1},{9,5},... | collective-permute-start | bytes 786440 | tf_op jit(solution)/shard_map/ppermute | solution.py:36
  6.8 4.3 %collective-permute-done.1 = bf16[256,512]{1,0:T(8,128)(2,1)S(1)} collective-permute-done((bf16[256,512]{1,0:T(8,128)(2,1)}, bf16[256,512]{1,0:T(8,128)(2,1)S(1)}, u32[]{:S(2)}, u32[]{:S(2)}) %collective-permute-start.1) | collective-permute-done | bytes 262176 | tf_op jit(solution)/shard_map/ppermute | solution.py:36
  11.1 2.0 %collective-permute-start.3 = (bf16[256,512]{1,0:T(8,128)(2,1)S(1)}, bf16[256,512]{1,0:T(8,128)(2,1)S(1)}, u32[]{:S(2)}, u32[]{:S(2)}) collective-permute-start(bf16[256,512]{1,0:T(8,128)(2,1)S(1)} %collective-permute-done.1), channel_id=1, source_target_pairs={{4,0},{8,4},{12,8},{14,12},{10,14},{6,10},{2,6},{0,2},{5,1},{9,5},... | collective-permute-start | bytes 786440 | tf_op jit(solution)/shard_map/ppermute | solution.py:36
  13.2 3.5 %collective-permute-done.22 = bf16[256,512]{1,0:T(8,128)(2,1)S(1)} collective-permute-done((bf16[256,512]{1,0:T(8,128)(2,1)}, bf16[256,512]{1,0:T(8,128)(2,1)S(1)}, u32[]{:S(2)}, u32[]{:S(2)}) %collective-permute-start.22) | collective-permute-done | bytes 262176 | tf_op jit(solution)/shard_map/ppermute | solution.py:36
  18.9 3.4 %collective-permute-done.3 = bf16[256,512]{1,0:T(8,128)(2,1)S(1)} collective-permute-done((bf16[256,512]{1,0:T(8,128)(2,1)S(1)}, bf16[256,512]{1,0:T(8,128)(2,1)S(1)}, u32[]{:S(2)}, u32[]{:S(2)}) %collective-permute-start.3) | collective-permute-done | bytes 262176 | tf_op jit(solution)/shard_map/ppermute | solution.py:36
  24.4 3.5 %collective-permute-done.24 = bf16[256,512]{1,0:T(8,128)(2,1)S(1)} collective-permute-done((bf16[256,512]{1,0:T(8,128)(2,1)S(1)}, bf16[256,512]{1,0:T(8,128)(2,1)S(1)}, u32[]{:S(2)}, u32[]{:S(2)}) %collective-permute-start.24) | collective-permute-done | bytes 262176 | tf_op jit(solution)/shard_map/ppermute | solution.py:36
  30.2 3.3 %collective-permute-done.5 = bf16[256,512]{1,0:T(8,128)(2,1)S(1)} collective-permute-done((bf16[256,512]{1,0:T(8,128)(2,1)S(1)}, bf16[256,512]{1,0:T(8,128)(2,1)S(1)}, u32[]{:S(2)}, u32[]{:S(2)}) %collective-permute-start.5) | collective-permute-done | bytes 262176 | tf_op jit(solution)/shard_map/ppermute | solution.py:36
  33.5 2.1 %collective-permute-start.7 = (bf16[128,512]{1,0:T(8,128)(2,1)S(1)}, bf16[128,512]{1,0:T(8,128)(2,1)S(1)}, u32[]{:S(2)}, u32[]{:S(2)}) collective-permute-start(bf16[128,512]{1,0:T(8,128)(2,1)S(1)} %slice.108), channel_id=1, source_target_pairs={{4,0},{8,4},{12,8},{14,12},{10,14},{6,10},{2,6},{0,2},{5,1},{9,5},... | collective-permute-start | bytes 393224 | tf_op jit(solution)/shard_map/ppermute | solution.py:39
  35.8 3.4 %collective-permute-done.26 = bf16[256,512]{1,0:T(8,128)(2,1)S(1)} collective-permute-done((bf16[256,512]{1,0:T(8,128)(2,1)S(1)}, bf16[256,512]{1,0:T(8,128)(2,1)S(1)}, u32[]{:S(2)}, u32[]{:S(2)}) %collective-permute-start.26) | collective-permute-done | bytes 262176 | tf_op jit(solution)/shard_map/ppermute | solution.py:36
  39.2 2.1 %collective-permute-start.28 = (bf16[128,512]{1,0:T(8,128)(2,1)S(1)}, bf16[128,512]{1,0:T(8,128)(2,1)S(1)}, u32[]{:S(2)}, u32[]{:S(2)}) collective-permute-start(bf16[128,512]{1,0:T(8,128)(2,1)S(1)} %slice.116), channel_id=1, source_target_pairs={{4,0},{8,4},{12,8},{14,12},{10,14},{6,10},{2,6},{0,2},{5,1},{9,5},... | collective-permute-start | bytes 393224 | tf_op jit(solution)/shard_map/ppermute | solution.py:39
  44.2 2.2 %collective-permute-done.27 = bf16[128,512]{1,0:T(8,128)(2,1)S(1)} collective-permute-done((bf16[128,512]{1,0:T(8,128)(2,1)S(1)}, bf16[128,512]{1,0:T(8,128)(2,1)S(1)}, u32[]{:S(2)}, u32[]{:S(2)}) %collective-permute-start.27) | collective-permute-done | bytes 131104 | tf_op jit(solution)/shard_map/ppermute | solution.py:38
  49.5 4.0 %fusion.1 = f32[512,1792]{1,0:T(8,128)S(1)} fusion(bf16[1792,2048]{1,0:T(8,128)(2,1)S(1)} %bitcast.7, bf16[256,2048]{1,0:T(8,128)(2,1)S(1)} %collective-permute-done.29, bf16[256,2048]{1,0:T(8,128)(2,1)S(1)} %get-tuple-element.18), kind=kOutput, calls=%fused_computation.21 | convolution fusion | flops 3762290688 | bytes 13107200 | tf_op jit(solution)/shard_map/dot_general | solution.py:106
  53.9 3.9 %fusion.10 = f32[512,1792]{1,0:T(8,128)S(1)} fusion(bf16[2048,1792]{1,0:T(8,128)(2,1)S(1)} %bitcast.9, bf16[256,2048]{1,0:T(8,128)(2,1)S(1)} %collective-permute-done.8, bf16[256,2048]{1,0:T(8,128)(2,1)S(1)} %get-tuple-element.30), kind=kOutput, calls=%fused_computation.76 | convolution fusion | flops 3762290688 | bytes 13107200 | tf_op jit(solution)/shard_map/dot_general | solution.py:106
  58.4 7.0 %fusion.11 = f32[512,1792]{1,0:T(8,128)S(1)} fusion(bf16[2048,1792]{1,0:T(8,128)(2,1)} %param.6, bf16[256,2048]{1,0:T(8,128)(2,1)S(1)} %collective-permute-done.8, bf16[256,2048]{1,0:T(8,128)(2,1)S(1)} %get-tuple-element.30), kind=kOutput, calls=%fused_computation.77 | convolution fusion | flops 3762290688 | bytes 13107200 | tf_op jit(solution)/shard_map/dot_general | solution.py:106
  65.7 2.3 %collective-permute-done.9 = bf16[256,1792]{1,0:T(8,128)(2,1)S(1)} collective-permute-done((bf16[256,1792]{1,0:T(8,128)(2,1)S(1)}, bf16[256,1792]{1,0:T(8,128)(2,1)S(1)}, u32[]{:S(2)}, u32[]{:S(2)}) %collective-permute-start.9) | collective-permute-done | bytes 917536 | tf_op jit(solution)/shard_map/ppermute | solution.py:26
  72.0 4.3 %convolution_convert_fusion.3 = bf16[512,2048]{1,0:T(8,128)(2,1)S(1)} fusion(bf16[1792,2048]{1,0:T(8,128)(2,1)S(1)} %bitcast.7, bf16[256,1792]{1,0:T(8,128)(2,1)S(1)} %collective-permute-done.11, bf16[256,1792]{1,0:T(8,128)(2,1)S(1)} %get-tuple-element.7), kind=kOutput, calls=%fused_computation.4 | convolution fusion | flops 3762814976 | bytes 11272192 | tf_op jit(solution)/shard_map/dot_general | solution.py:106
  79.5 5.5 %fusion.2 = f32[512,2048]{1,0:T(8,128)} fusion(bf16[2048,1792]{1,0:T(8,128)(2,1)S(1)} %bitcast.11, bf16[256,1792]{1,0:T(8,128)(2,1)S(1)} %collective-permute-done.32, bf16[256,1792]{1,0:T(8,128)(2,1)S(1)} %get-tuple-element.6), kind=kOutput, calls=%fused_computation.22 | convolution fusion | flops 3761766400 | bytes 13369344 | tf_op jit(solution)/shard_map/dot_general | solution.py:106
  85.0 8.6 %add_convert_fusion = bf16[512,2048]{1,0:T(8,128)(2,1)S(1)} fusion(f32[512,2048]{1,0:T(8,128)} %fusion.2, bf16[2048,1792]{1,0:T(8,128)(2,1)} %param.6, bf16[256,1792]{1,0:T(8,128)(2,1)S(1)} %collective-permute-done.31, bf16[256,1792]{1,0:T(8,128)(2,1)S(1)} %get-tuple-element.5), kind=kOutput, calls=%fused_computation.3 | convolution fusion | flops 3763863552 | bytes 15466496 | tf_op jit(solution)/shard_map/dot_general | solution.py:106
  95.4 2.4 %constant_dynamic-update-slice_fusion.8 = bf16[256,4096]{1,0:T(8,128)(2,1)} fusion(bf16[256,4096]{1,0:T(8,128)(2,1)} %get-tuple-element.29, bf16[256,2048]{1,0:T(8,128)(2,1)} %collective-permute-done.12, s32[]{:T(128)S(6)} %select_n.149), kind=kLoop, calls=%fused_computation.59 | loop fusion | bytes 2097156 | tf_op jit(solution)/shard_map/dynamic_update_slice | solution.py:77
  110.1 6.6 %collective-permute-done.14 = bf16[256,512]{1,0:T(8,128)(2,1)S(1)} collective-permute-done((bf16[256,512]{1,0:T(8,128)(2,1)S(1)}, bf16[256,512]{1,0:T(8,128)(2,1)S(1)}, u32[]{:S(2)}, u32[]{:S(2)}) %collective-permute-start.14) | collective-permute-done | bytes 262176 | tf_op jit(solution)/shard_map/ppermute | solution.py:100
  118.1 4.2 %collective-permute-done.35 = bf16[256,512]{1,0:T(8,128)(2,1)S(1)} collective-permute-done((bf16[256,512]{1,0:T(8,128)(2,1)S(1)}, bf16[256,512]{1,0:T(8,128)(2,1)S(1)}, u32[]{:S(2)}, u32[]{:S(2)}) %collective-permute-start.35) | collective-permute-done | bytes 262176 | tf_op jit(solution)/shard_map/ppermute | solution.py:100
  122.8 6.1 %convolution_convert_fusion = bf16[1792,2048]{1,0:T(8,128)(2,1)} fusion(bf16[256,2048]{1,0:T(8,128)(2,1)S(1)} %copy-done.13, bf16[256,2048]{1,0:T(8,128)(2,1)S(1)} %copy-done.1, bf16[256,1792]{1,0:T(8,128)(2,1)S(1)} %copy-done.19, bf16[256,1792]{1,0:T(8,128)(2,1)S(1)} %copy-done.7), kind=kOutput, calls=%fused_computation | convolution fusion | flops 3769630720 | bytes 11272192 | tf_op jit(solution)/shard_map/dot_general | solution.py:106
  133.8 6.1 %convolution_convert_fusion.2 = bf16[2048,1792]{1,0:T(8,128)(2,1)} fusion(bf16[256,1792]{1,0:T(8,128)(2,1)S(1)} %copy-done.17, bf16[256,1792]{1,0:T(8,128)(2,1)S(1)} %copy-done.5, bf16[256,2048]{1,0:T(8,128)(2,1)S(1)} %copy-done.11, bf16[256,2048]{1,0:T(8,128)(2,1)S(1)} %get-tuple-element.30), kind=kOutput, calls=%fused_computation.2 | convolution fusion | flops 3769630720 | bytes 11272192 | tf_op jit(solution)/shard_map/dot_general | solution.py:106
  145.3 6.1 %convolution_convert_fusion.1 = bf16[2048,1792]{1,0:T(8,128)(2,1)} fusion(bf16[256,1792]{1,0:T(8,128)(2,1)S(1)} %copy-done.15, bf16[256,1792]{1,0:T(8,128)(2,1)S(1)} %copy-done.3, bf16[256,2048]{1,0:T(8,128)(2,1)S(1)} %copy-done.11, bf16[256,2048]{1,0:T(8,128)(2,1)S(1)} %get-tuple-element.30), kind=kOutput, calls=%fused_computation.1 | convolution fusion | flops 3769630720 | bytes 11272192 | tf_op jit(solution)/shard_map/dot_general | solution.py:106
  (173 shorter events, 52.8 us)
Async XLA Ops:
  0.6 10.4 %collective-permute-start.1 = (bf16[256,512]{1,0:T(8,128)(2,1)}, bf16[256,512]{1,0:T(8,128)(2,1)S(1)}, u32[]{:S(2)}, u32[]{:S(2)}) collective-permute-start(bf16[256,512]{1,0:T(8,128)(2,1)} %param.5), channel_id=1, source_target_pairs={{4,0},{8,4},{12,8},{14,12},{10,14},{6,10},{2,6},{0,2},{5,1},{9,5},... | collective-permute-start | bytes 786440 | tf_op jit(solution)/shard_map/ppermute | solution.py:36
  3.8 12.9 %collective-permute-start.22 = (bf16[256,512]{1,0:T(8,128)(2,1)}, bf16[256,512]{1,0:T(8,128)(2,1)S(1)}, u32[]{:S(2)}, u32[]{:S(2)}) collective-permute-start(bf16[256,512]{1,0:T(8,128)(2,1)} %param.9), channel_id=1, source_target_pairs={{4,0},{8,4},{12,8},{14,12},{10,14},{6,10},{2,6},{0,2},{5,1},{9,5},... | collective-permute-start | bytes 786440 | tf_op jit(solution)/shard_map/ppermute | solution.py:36
  5.7 13.0 %collective-permute-start.21 = (bf16[256,512]{1,0:T(8,128)(2,1)}, bf16[256,512]{1,0:T(8,128)(2,1)S(1)}, u32[]{:S(2)}, u32[]{:S(2)}) collective-permute-start(bf16[256,512]{1,0:T(8,128)(2,1)} %param.9), channel_id=1, source_target_pairs={{0,4},{4,8},{8,12},{12,14},{14,10},{10,6},{6,2},{2,0},{1,5},{5,9},... | collective-permute-start | bytes 786440 | tf_op jit(solution)/shard_map/ppermute | solution.py:35
  11.1 11.2 %collective-permute-start.3 = (bf16[256,512]{1,0:T(8,128)(2,1)S(1)}, bf16[256,512]{1,0:T(8,128)(2,1)S(1)}, u32[]{:S(2)}, u32[]{:S(2)}) collective-permute-start(bf16[256,512]{1,0:T(8,128)(2,1)S(1)} %collective-permute-done.1), channel_id=1, source_target_pairs={{4,0},{8,4},{12,8},{14,12},{10,14},{6,10},{2,6},{0,2},{5,1},{9,5},... | collective-permute-start | bytes 786440 | tf_op jit(solution)/shard_map/ppermute | solution.py:36
  13.1 11.2 %collective-permute-start.2 = (bf16[256,512]{1,0:T(8,128)(2,1)S(1)}, bf16[256,512]{1,0:T(8,128)(2,1)S(1)}, u32[]{:S(2)}, u32[]{:S(2)}) collective-permute-start(bf16[256,512]{1,0:T(8,128)(2,1)S(1)} %collective-permute-done), channel_id=1, source_target_pairs={{0,4},{4,8},{8,12},{12,14},{14,10},{10,6},{6,2},{2,0},{1,5},{5,9},... | collective-permute-start | bytes 786440 | tf_op jit(solution)/shard_map/ppermute | solution.py:35
  16.7 11.2 %collective-permute-start.24 = (bf16[256,512]{1,0:T(8,128)(2,1)S(1)}, bf16[256,512]{1,0:T(8,128)(2,1)S(1)}, u32[]{:S(2)}, u32[]{:S(2)}) collective-permute-start(bf16[256,512]{1,0:T(8,128)(2,1)S(1)} %collective-permute-done.22), channel_id=1, source_target_pairs={{4,0},{8,4},{12,8},{14,12},{10,14},{6,10},{2,6},{0,2},{5,1},{9,5},... | collective-permute-start | bytes 786440 | tf_op jit(solution)/shard_map/ppermute | solution.py:36
  18.7 11.2 %collective-permute-start.23 = (bf16[256,512]{1,0:T(8,128)(2,1)S(1)}, bf16[256,512]{1,0:T(8,128)(2,1)S(1)}, u32[]{:S(2)}, u32[]{:S(2)}) collective-permute-start(bf16[256,512]{1,0:T(8,128)(2,1)S(1)} %collective-permute-done.21), channel_id=1, source_target_pairs={{0,4},{4,8},{8,12},{12,14},{14,10},{10,6},{6,2},{2,0},{1,5},{5,9},... | collective-permute-start | bytes 786440 | tf_op jit(solution)/shard_map/ppermute | solution.py:35
  22.3 11.2 %collective-permute-start.5 = (bf16[256,512]{1,0:T(8,128)(2,1)S(1)}, bf16[256,512]{1,0:T(8,128)(2,1)S(1)}, u32[]{:S(2)}, u32[]{:S(2)}) collective-permute-start(bf16[256,512]{1,0:T(8,128)(2,1)S(1)} %collective-permute-done.3), channel_id=1, source_target_pairs={{4,0},{8,4},{12,8},{14,12},{10,14},{6,10},{2,6},{0,2},{5,1},{9,5},... | collective-permute-start | bytes 786440 | tf_op jit(solution)/shard_map/ppermute | solution.py:36
  24.3 11.3 %collective-permute-start.4 = (bf16[256,512]{1,0:T(8,128)(2,1)S(1)}, bf16[256,512]{1,0:T(8,128)(2,1)S(1)}, u32[]{:S(2)}, u32[]{:S(2)}) collective-permute-start(bf16[256,512]{1,0:T(8,128)(2,1)S(1)} %collective-permute-done.2), channel_id=1, source_target_pairs={{0,4},{4,8},{8,12},{12,14},{14,10},{10,6},{6,2},{2,0},{1,5},{5,9},... | collective-permute-start | bytes 786440 | tf_op jit(solution)/shard_map/ppermute | solution.py:35
  27.9 11.2 %collective-permute-start.26 = (bf16[256,512]{1,0:T(8,128)(2,1)S(1)}, bf16[256,512]{1,0:T(8,128)(2,1)S(1)}, u32[]{:S(2)}, u32[]{:S(2)}) collective-permute-start(bf16[256,512]{1,0:T(8,128)(2,1)S(1)} %collective-permute-done.24), channel_id=1, source_target_pairs={{4,0},{8,4},{12,8},{14,12},{10,14},{6,10},{2,6},{0,2},{5,1},{9,5},... | collective-permute-start | bytes 786440 | tf_op jit(solution)/shard_map/ppermute | solution.py:36
  30.0 11.3 %collective-permute-start.25 = (bf16[256,512]{1,0:T(8,128)(2,1)S(1)}, bf16[256,512]{1,0:T(8,128)(2,1)S(1)}, u32[]{:S(2)}, u32[]{:S(2)}) collective-permute-start(bf16[256,512]{1,0:T(8,128)(2,1)S(1)} %collective-permute-done.23), channel_id=1, source_target_pairs={{0,4},{4,8},{8,12},{12,14},{14,10},{10,6},{6,2},{2,0},{1,5},{5,9},... | collective-permute-start | bytes 786440 | tf_op jit(solution)/shard_map/ppermute | solution.py:35
  53.7 12.1 %collective-permute-start.30 = (bf16[256,1792]{1,0:T(8,128)(2,1)S(1)}, bf16[256,1792]{1,0:T(8,128)(2,1)S(1)}, u32[]{:S(2)}, u32[]{:S(2)}) collective-permute-start(bf16[256,1792]{1,0:T(8,128)(2,1)S(1)} %slice.145), channel_id=1, source_target_pairs={{0,1},{1,0},{2,3},{3,2},{4,5},{5,4},{6,7},{7,6},{8,9},{9,8},{10,11... | collective-permute-start | bytes 2752520 | tf_op jit(solution)/shard_map/ppermute | solution.py:26
  69.6 15.4 %collective-permute-start.31 = (bf16[256,1792]{1,0:T(8,128)(2,1)S(1)}, bf16[256,1792]{1,0:T(8,128)(2,1)S(1)}, u32[]{:S(2)}, u32[]{:S(2)}) collective-permute-start(bf16[256,1792]{1,0:T(8,128)(2,1)S(1)} %get-tuple-element.5), channel_id=1, source_target_pairs={{0,1},{1,0},{2,3},{3,2},{4,5},{5,4},{6,7},{7,6},{8,9},{9,8},{10,11... | collective-permute-start | bytes 2752520 | tf_op jit(solution)/shard_map/ppermute | solution.py:26
  79.2 16.2 %collective-permute-start.12 = (bf16[256,2048]{1,0:T(8,128)(2,1)}, bf16[256,2048]{1,0:T(8,128)(2,1)}, u32[]{:S(2)}, u32[]{:S(2)}) collective-permute-start(bf16[256,2048]{1,0:T(8,128)(2,1)} %get-tuple-element.28), channel_id=1, source_target_pairs={{0,1},{1,0},{2,3},{3,2},{4,5},{5,4},{6,7},{7,6},{8,9},{9,8},{10,11... | collective-permute-start | bytes 3145736 | tf_op jit(solution)/shard_map/ppermute | solution.py:26
  105.6 23.3 %collective-permute-start.18 = (bf16[256,512]{1,0:T(8,128)(2,1)S(1)}, bf16[256,512]{1,0:T(8,128)(2,1)S(1)}, u32[]{:S(2)}, u32[]{:S(2)}) collective-permute-start(bf16[256,512]{1,0:T(8,128)(2,1)S(1)} %pad_maximum_fusion.14), channel_id=1, source_target_pairs={{4,0},{8,4},{12,8},{14,12},{10,14},{6,10},{2,6},{0,2},{5,1},{9,5},... | collective-permute-start | bytes 786440 | tf_op jit(solution)/shard_map/ppermute | solution.py:101
  107.9 14.4 %collective-permute-start.35 = (bf16[256,512]{1,0:T(8,128)(2,1)S(1)}, bf16[256,512]{1,0:T(8,128)(2,1)S(1)}, u32[]{:S(2)}, u32[]{:S(2)}) collective-permute-start(bf16[256,512]{1,0:T(8,128)(2,1)S(1)} %pad_maximum_fusion.15), channel_id=1, source_target_pairs={{0,4},{4,8},{8,12},{12,14},{14,10},{10,6},{6,2},{2,0},{1,5},{5,9},... | collective-permute-start | bytes 786440 | tf_op jit(solution)/shard_map/ppermute | solution.py:100
  109.8 22.2 %collective-permute-start.39 = (bf16[256,512]{1,0:T(8,128)(2,1)S(1)}, bf16[256,512]{1,0:T(8,128)(2,1)S(1)}, u32[]{:S(2)}, u32[]{:S(2)}) collective-permute-start(bf16[256,512]{1,0:T(8,128)(2,1)S(1)} %pad_maximum_fusion.16), channel_id=1, source_target_pairs={{4,0},{8,4},{12,8},{14,12},{10,14},{6,10},{2,6},{0,2},{5,1},{9,5},... | collective-permute-start | bytes 786440 | tf_op jit(solution)/shard_map/ppermute | solution.py:101
  117.7 11.2 %collective-permute-start.15 = (bf16[256,512]{1,0:T(8,128)(2,1)S(1)}, bf16[256,512]{1,0:T(8,128)(2,1)S(1)}, u32[]{:S(2)}, u32[]{:S(2)}) collective-permute-start(bf16[256,512]{1,0:T(8,128)(2,1)S(1)} %dynamic-slice_add_fusion.6), channel_id=1, source_target_pairs={{0,4},{4,8},{8,12},{12,14},{14,10},{10,6},{6,2},{2,0},{1,5},{5,9},... | collective-permute-start | bytes 786440 | tf_op jit(solution)/shard_map/ppermute | solution.py:100
  122.4 9.6 %collective-permute-start.36 = (bf16[256,512]{1,0:T(8,128)(2,1)S(1)}, bf16[256,512]{1,0:T(8,128)(2,1)S(1)}, u32[]{:S(2)}, u32[]{:S(2)}) collective-permute-start(bf16[256,512]{1,0:T(8,128)(2,1)S(1)} %dynamic-slice_add_fusion.2), channel_id=1, source_target_pairs={{0,4},{4,8},{8,12},{12,14},{14,10},{10,6},{6,2},{2,0},{1,5},{5,9},... | collective-permute-start | bytes 786440 | tf_op jit(solution)/shard_map/ppermute | solution.py:100
  130.2 10.5 %collective-permute-start.19 = (bf16[256,512]{1,0:T(8,128)(2,1)S(1)}, bf16[256,512]{1,0:T(8,128)(2,1)S(1)}, u32[]{:S(2)}, u32[]{:S(2)}) collective-permute-start(bf16[256,512]{1,0:T(8,128)(2,1)S(1)} %get-tuple-element.21), channel_id=1, source_target_pairs={{4,0},{8,4},{12,8},{14,12},{10,14},{6,10},{2,6},{0,2},{5,1},{9,5},... | collective-permute-start | bytes 786440 | tf_op jit(solution)/shard_map/ppermute | solution.py:101
  132.2 11.3 %collective-permute-start.40 = (bf16[256,512]{1,0:T(8,128)(2,1)S(1)}, bf16[256,512]{1,0:T(8,128)(2,1)S(1)}, u32[]{:S(2)}, u32[]{:S(2)}) collective-permute-start(bf16[256,512]{1,0:T(8,128)(2,1)S(1)} %get-tuple-element.9), channel_id=1, source_target_pairs={{4,0},{8,4},{12,8},{14,12},{10,14},{6,10},{2,6},{0,2},{5,1},{9,5},... | collective-permute-start | bytes 786440 | tf_op jit(solution)/shard_map/ppermute | solution.py:101
  140.0 11.4 %collective-permute-start.16 = (bf16[256,512]{1,0:T(8,128)(2,1)S(1)}, bf16[256,512]{1,0:T(8,128)(2,1)S(1)}, u32[]{:S(2)}, u32[]{:S(2)}) collective-permute-start(bf16[256,512]{1,0:T(8,128)(2,1)S(1)} %get-tuple-element.20), channel_id=1, source_target_pairs={{0,4},{4,8},{8,12},{12,14},{14,10},{10,6},{6,2},{2,0},{1,5},{5,9},... | collective-permute-start | bytes 786440 | tf_op jit(solution)/shard_map/ppermute | solution.py:100
  140.4 12.7 %collective-permute-start.37 = (bf16[256,512]{1,0:T(8,128)(2,1)S(1)}, bf16[256,512]{1,0:T(8,128)(2,1)S(1)}, u32[]{:S(2)}, u32[]{:S(2)}) collective-permute-start(bf16[256,512]{1,0:T(8,128)(2,1)S(1)} %get-tuple-element.8), channel_id=1, source_target_pairs={{0,4},{4,8},{8,12},{12,14},{14,10},{10,6},{6,2},{2,0},{1,5},{5,9},... | collective-permute-start | bytes 786440 | tf_op jit(solution)/shard_map/ppermute | solution.py:100
  141.8 9.6 %collective-permute-start.20 = (bf16[256,512]{1,0:T(8,128)(2,1)S(1)}, bf16[256,512]{1,0:T(8,128)(2,1)S(1)}, u32[]{:S(2)}, u32[]{:S(2)}) collective-permute-start(bf16[256,512]{1,0:T(8,128)(2,1)S(1)} %dynamic-slice_add_fusion.5), channel_id=1, source_target_pairs={{4,0},{8,4},{12,8},{14,12},{10,14},{6,10},{2,6},{0,2},{5,1},{9,5},... | collective-permute-start | bytes 786440 | tf_op jit(solution)/shard_map/ppermute | solution.py:101
  (44 other events, 340.3 us)

commit v2 on v1

v2 whole, which is shorter than its diff:
```python
import jax
import jax.numpy as jnp
from jax import lax
from jax.sharding import PartitionSpec as P

BF16 = jnp.bfloat16
F32 = jnp.float32


def hops(n):
    order = list(range(0, n, 2)) + list(range(n - 1, 0, -2))
    up = [(order[i], order[(i + 1) % n]) for i in range(n)]
    return up, [(b, a) for a, b in up]


class Ring:
    def __init__(self, n):
        self.n, self.m = n, n // 2
        self.up_hops, self.down_hops = hops(n)
        index = lax.axis_index("tp")
        self.core = lax.axis_index("dp")
        self.spot = jnp.where(lax.rem(index, 2) == 0, index // 2, n - 1 - index // 2)

    def up(self, value):
        return lax.ppermute(value, "tp", self.up_hops)

    def down(self, value):
        return lax.ppermute(value, "tp", self.down_hops)

    def index_at(self, distance):
        place = lax.rem(self.spot + distance + 2 * self.n, self.n)
        return jnp.where(place < self.m, 2 * place, 2 * (self.n - 1 - place) + 1)

    def pair(self, distance):
        first, second = self.index_at(distance), self.index_at(distance - self.m)
        mine = first // self.m == self.core
        return mine, jnp.where(mine, first, second) - self.core * self.m


def swap_cores(value):
    return lax.ppermute(value, "dp", [(0, 1), (1, 0)])


def after(values, done):
    return lax.optimization_barrier((values, done))[0]


def dot(left, right, left_dim, right_dim):
    return lax.dot_general(left, right, (((left_dim,), (right_dim,)), ((), ())), preferred_element_type=F32)


class Gather:
    def __init__(self, ring, own, far_up):
        self.ring, self.far_up = ring, far_up
        self.blocks = {0: own}
        shape = (own.shape[0], own.shape[1] * ring.m)
        self.own, self.got = jnp.zeros(shape, own.dtype), jnp.zeros(shape, own.dtype)
        self.step = 0

    def advance(self, done):
        ring, s = self.ring, self.step
        behind, ahead = after((self.blocks[-s], self.blocks[s]), done)
        s = self.step = s + 1
        if s < ring.m:
            self.blocks[-s], self.blocks[s] = ring.up(behind), ring.down(ahead)
        else:
            self.blocks[-s] = self.blocks[s] = ring.up(behind) if self.far_up else ring.down(ahead)
        return behind

    def swap(self, step, mark):
        ring = self.ring
        width = self.blocks[0].shape[1]
        made = []
        for d in range(1, ring.m + 1):
            if max(d, ring.m - d) == step:
                mine, block = ring.pair(d)
                first, second = after((self.blocks[d], self.blocks[d - ring.m]), mark)
                keep, send = jnp.where(mine, first, second), jnp.where(mine, second, first)
                self.own = lax.dynamic_update_slice(self.own, keep, (0, block * width))
                self.got = lax.dynamic_update_slice(self.got, swap_cores(send), (0, block * width))
                made.append(send)
        return made


class Terms:
    def __init__(self, ring, term_of):
        self.ring, self.term_of, self.made = ring, term_of, {}

    def work_out(self, pairs, mark):
        results = []
        for d in pairs:
            if d in self.made or d <= 0:
                continue
            mine, block = self.ring.pair(d)
            own, other = self.term_of(block, mark)
            got = swap_cores(other)
            self.made[d] = (mine, own, got)
            self.made[d - self.ring.m] = (mine, got, own)
            results.append(other)
        return results

    def __getitem__(self, distance):
        return jnp.where(*self.made[distance])


class Sum:
    def __init__(self, ring, terms, far_up):
        self.ring, self.terms, self.far_up = ring, terms, far_up
        self.distance = ring.m
        self.ahead = self.behind = None

    def advance(self, done):
        ring, distance = self.ring, self.distance
        self.distance -= 1
        if distance == ring.m:
            far = after(self.terms[distance], done)
            if self.far_up:
                self.ahead = ring.up(far)
            else:
                self.behind = ring.down(far)
            return far
        ahead, behind = self.terms[distance], self.terms[-distance]
        if self.ahead is not None:
            ahead = ahead + self.ahead
        if self.behind is not None:
            behind = behind + self.behind
        ahead, behind = after((ahead, behind), done)
        self.ahead, self.behind = ring.up(ahead), ring.down(behind)
        return behind

    def total(self):
        return self.terms[0].astype(F32) + self.ahead.astype(F32) + self.behind.astype(F32)


def body(n, tokens, gate_weight, up_weight, down_weight, out_grad):
    ring = Ring(n)
    m, rows, width = n // 2, tokens.shape[0], tokens.shape[1]

    def rows_of(weight, block):
        return lax.dynamic_slice_in_dim(weight, block * width, width, 0)

    def columns_of(weight, block):
        return lax.dynamic_slice_in_dim(weight, block * width, width, 1)

    t, g = Gather(ring, tokens, True), Gather(ring, out_grad, False)
    done = []
    for step in range(1, m + 1):
        mark = t.advance(done)
        done = t.swap(step - 1, mark)
        mark = g.advance(done)
        done = g.swap(step - 1, mark)
    t.swap(m, done)
    gate_own, up_own = dot(t.own, gate_weight, 1, 0), dot(t.own, up_weight, 1, 0)
    t_got = after(t.got, (gate_own, up_own))
    gate_other, up_other = dot(t_got, gate_weight, 1, 0).astype(BF16), dot(t_got, up_weight, 1, 0).astype(BF16)
    gate_got, up_got = swap_cores(gate_other), swap_cores(up_other)
    g.swap(m, gate_own)
    g_own, g_got = after((g.own, g.got), (gate_other, up_other))
    grad_other = dot(g_got, down_weight, 1, 1).astype(BF16)
    grad_got = swap_cores(grad_other)
    grad_own = dot(g_own, down_weight, 1, 1)

    gate_value, up_value = gate_own + gate_got.astype(F32), up_own + up_got.astype(F32)
    sigmoid_gate = jax.nn.sigmoid(gate_value)
    activated = gate_value * sigmoid_gate
    slope = up_value * sigmoid_gate * (1.0 + gate_value * (1.0 - sigmoid_gate))
    hidden = (activated * up_value).astype(BF16)
    activated, slope, hidden = lax.optimization_barrier((activated, slope, hidden))
    hidden_got = swap_cores(hidden)
    hidden_grad = after(grad_own, hidden) + grad_got.astype(F32)
    gate_grad, up_grad = (hidden_grad * slope).astype(BF16), (hidden_grad * activated).astype(BF16)
    gate_grad, up_grad = lax.optimization_barrier((gate_grad, up_grad))
    gate_grad_got, up_grad_got = swap_cores(gate_grad), swap_cores(up_grad)
    hidden_both = jnp.concatenate([hidden, hidden_got], 0)
    gate_both = jnp.concatenate([gate_grad, gate_grad_got], 0)
    up_both = jnp.concatenate([up_grad, up_grad_got], 0)

    def output_term(block, mark):
        h = after(hidden_both, mark)
        both = dot(h, columns_of(down_weight, block), 1, 0).astype(BF16)
        return both[:rows], both[rows:]

    def input_term(block, mark):
        a, b = after((gate_both, up_both), mark)
        both = (dot(a, rows_of(gate_weight, block), 1, 1) + dot(b, rows_of(up_weight, block), 1, 1)).astype(BF16)
        return both[:rows], both[rows:]

    tokens_half = jnp.concatenate([t.own, t.got], 0)
    grad_half = jnp.concatenate([g.own, g.got], 0)
    wgrads = []
    pieces = [
        lambda mark: dot(after(hidden_both, mark), grad_half, 0, 0).astype(BF16),
        lambda mark: dot(tokens_half, after(gate_both, mark), 0, 0).astype(BF16),
        lambda mark: dot(tokens_half, after(up_both, mark), 0, 0).astype(BF16),
    ]

    def wgrad_work(mark):
        wgrads.append(pieces[len(wgrads)](mark))
        return [wgrads[-1]]

    o, i = Terms(ring, output_term), Terms(ring, input_term)
    o.work_out([m], [])
    i.work_out([m], o.made[m][1])
    o_sum, i_sum = Sum(ring, o, True), Sum(ring, i, False)
    mark = o_sum.advance([])
    done = o.work_out([m - 1, 1], (mark, i.made[m][1]))
    mark = i_sum.advance(done)
    done = i.work_out([m - 1], mark)
    for distance in range(m - 1, 0, -1):
        mark = o_sum.advance(done)
        done = i.work_out([m - distance], mark)
        if distance <= 2:
            done += wgrad_work(mark)
        mark = i_sum.advance(done)
        pairs = [distance - 1, m - distance + 1]
        done = o.work_out(pairs, mark) + i.work_out(pairs[:1], mark)
        if distance == 1:
            wgrad_work(mark)
    output, input_grad = o_sum.total(), i_sum.total()
    return output.astype(BF16), input_grad.astype(BF16), wgrads[1], wgrads[2], wgrads[0]


def solution(mesh):
    n = mesh.shape["tp"]
    rows = P(("rep", "dp"), "tp")
    in_specs = (rows, P("dp", "tp"), P("dp", "tp"), P("tp", "dp"), rows)
    out_specs = (rows, rows, rows, rows, P("tp", ("rep", "dp")))

    def call(*args):
        return body(n, *args)

    return jax.shard_map(call, mesh=mesh, in_specs=in_specs, out_specs=out_specs, check_vma=False)
```

time: 154 us -> 128 us (0.83)
  local copies, waits for them, and re-layouts: 11.3 us -> 3.01 us
  matrix products: 51.7 us -> 44.4 us
  waiting for transfers between devices: 43.3 us -> 37.3 us
  other arithmetic: 9 us -> 4.77 us
    dot_general x9 -> x21, matrix products: 51.7 us -> 44.4 us  [dot(): lax.dot_general(left, right, (((left_dim,), (right_dim,)), ((), ())), pre...]
    add x8, other arithmetic: 4.96 us -> 0.34 us  [the longest x5 0.23 us: advance(): behind = behind + self.behind]
    dynamic_update_slice x16 -> x8, local copies, waits for them, and re-layouts: 4.04 us -> 0.21 us  [swap(): lax.dynamic_update_slice(self.got, swap_cores(send), (0, block * width))]
    slice x11 -> x8, local copies, waits for them, and re-layouts: 3.98 us -> 0.15 us  [the longest x4 0.08 us: output_term(): return (both[:rows], both[rows:])]
    ppermute x10 -> x22, waiting for transfers between devices: 6.01 us -> 2.32 us  [swap_cores(): return lax.ppermute(value, 'dp', [(0, 1), (1, 0)])]
    ppermute x32 -> x28, starting transfers between devices: 34.8 us -> 32 us  [the longest x14 22.3 us: up(): return lax.ppermute(value, 'tp', self.up_hops)]
    ppermute x10 -> x22, starting transfers between devices: 2.67 us -> 5.13 us  [swap_cores(): return lax.ppermute(value, 'dp', [(0, 1), (1, 0)])]
    ppermute x32 -> x28, waiting for transfers between devices: 37.2 us -> 35 us  [the longest x14 18.7 us: down(): return lax.ppermute(value, 'tp', self.down_hops)]
  transfers between devices with their start and end apart: 42 -> 50, of which waited for: 17 -> 19; matrix products, arithmetic and copies ran while one was open for 45% -> 39% of each run, Pallas kernels for 0% -> 0%
where the time goes in v2:
time: 128 us
  matrix products  44.4 us (35%)
  waiting for transfers between devices  37.3 us (29%)
  starting transfers between devices  37.1 us (29%)
  other arithmetic  4.77 us (4%)
  local copies, waits for them, and re-layouts  3.01 us (2%)
  between operations  1.41 us (1%)
    dot_general x21, matrix products, dot(): lax.dot_general(left, right, (((left_dim,), (right_dim,)), ((), ())), pre...  44.4 us
    ppermute x14, starting transfers between devices, up(): return lax.ppermute(value, 'tp', self.up_hops)  22.3 us
    ppermute x14, waiting for transfers between devices, down(): return lax.ppermute(value, 'tp', self.down_hops)  18.7 us
    ppermute x14, waiting for transfers between devices, up(): return lax.ppermute(value, 'tp', self.up_hops)  16.3 us
    ppermute x14, starting transfers between devices, down(): return lax.ppermute(value, 'tp', self.down_hops)  9.65 us
    ppermute x22, starting transfers between devices, swap_cores(): return lax.ppermute(value, 'dp', [(0, 1), (1, 0)])  5.13 us
  transfers between devices with their start and end apart: 50, of which 19 were waited for; matrix products, arithmetic and copies ran while one was open for 39% of the time, Pallas kernels for 0%

profile of v2, /device:TPU:0, one launch (start us, length us, event | category | flops | bytes accessed | tf_op | source)
XLA Modules:
  0.0 128.0 jit_solution(4331174017229603492)
XLA Ops:
  0.6 3.1 %collective-permute-start = (bf16[256,512]{1,0:T(8,128)(2,1)}, bf16[256,512]{1,0:T(8,128)(2,1)S(1)}, u32[]{:S(2)}, u32[]{:S(2)}) collective-permute-start(bf16[256,512]{1,0:T(8,128)(2,1)} %param.5), channel_id=1, source_target_pairs={{0,4},{4,8},{8,12},{12,14},{14,10},{10,6},{6,2},{2,0},{1,5},{5,9},... | collective-permute-start | bytes 786440 | tf_op jit(solution)/shard_map/ppermute | solution.py:25
  3.7 2.0 %collective-permute-start.6 = (bf16[256,512]{1,0:T(8,128)(2,1)}, bf16[256,512]{1,0:T(8,128)(2,1)S(1)}, u32[]{:S(2)}, u32[]{:S(2)}) collective-permute-start(bf16[256,512]{1,0:T(8,128)(2,1)} %param.9), channel_id=1, source_target_pairs={{0,4},{4,8},{8,12},{12,14},{14,10},{10,6},{6,2},{2,0},{1,5},{5,9},... | collective-permute-start | bytes 786440 | tf_op jit(solution)/shard_map/ppermute | solution.py:25
  5.7 5.3 %collective-permute-done = bf16[256,512]{1,0:T(8,128)(2,1)S(1)} collective-permute-done((bf16[256,512]{1,0:T(8,128)(2,1)}, bf16[256,512]{1,0:T(8,128)(2,1)S(1)}, u32[]{:S(2)}, u32[]{:S(2)}) %collective-permute-start) | collective-permute-done | bytes 262176 | tf_op jit(solution)/shard_map/ppermute | solution.py:25
  11.0 2.2 %collective-permute-done.1 = bf16[256,512]{1,0:T(8,128)(2,1)S(1)} collective-permute-done((bf16[256,512]{1,0:T(8,128)(2,1)}, bf16[256,512]{1,0:T(8,128)(2,1)S(1)}, u32[]{:S(2)}, u32[]{:S(2)}) %collective-permute-start.1) | collective-permute-done | bytes 262176 | tf_op jit(solution)/shard_map/ppermute | solution.py:28
  13.2 2.0 %collective-permute-start.3 = (bf16[256,512]{1,0:T(8,128)(2,1)S(1)}, bf16[256,512]{1,0:T(8,128)(2,1)S(1)}, u32[]{:S(2)}, u32[]{:S(2)}) collective-permute-start(bf16[256,512]{1,0:T(8,128)(2,1)S(1)} %collective-permute-done), channel_id=1, source_target_pairs={{0,4},{4,8},{8,12},{12,14},{14,10},{10,6},{6,2},{2,0},{1,5},{5,9},... | collective-permute-start | bytes 786440 | tf_op jit(solution)/shard_map/ppermute | solution.py:25
  16.6 2.2 %collective-permute-done.7 = bf16[256,512]{1,0:T(8,128)(2,1)S(1)} collective-permute-done((bf16[256,512]{1,0:T(8,128)(2,1)}, bf16[256,512]{1,0:T(8,128)(2,1)S(1)}, u32[]{:S(2)}, u32[]{:S(2)}) %collective-permute-start.7) | collective-permute-done | bytes 262176 | tf_op jit(solution)/shard_map/ppermute | solution.py:28
  18.8 2.0 %collective-permute-start.9 = (bf16[256,512]{1,0:T(8,128)(2,1)S(1)}, bf16[256,512]{1,0:T(8,128)(2,1)S(1)}, u32[]{:S(2)}, u32[]{:S(2)}) collective-permute-start(bf16[256,512]{1,0:T(8,128)(2,1)S(1)} %collective-permute-done.6), channel_id=1, source_target_pairs={{0,4},{4,8},{8,12},{12,14},{14,10},{10,6},{6,2},{2,0},{1,5},{5,9},... | collective-permute-start | bytes 786440 | tf_op jit(solution)/shard_map/ppermute | solution.py:25
  20.8 3.6 %collective-permute-done.2 = bf16[256,512]{1,0:T(8,128)(2,1)S(1)} collective-permute-done((bf16[256,512]{1,0:T(8,128)(2,1)S(1)}, bf16[256,512]{1,0:T(8,128)(2,1)S(1)}, u32[]{:S(2)}, u32[]{:S(2)}) %collective-permute-start.2) | collective-permute-done | bytes 262176 | tf_op jit(solution)/shard_map/ppermute | solution.py:28
  26.7 3.3 %collective-permute-done.8 = bf16[256,512]{1,0:T(8,128)(2,1)S(1)} collective-permute-done((bf16[256,512]{1,0:T(8,128)(2,1)S(1)}, bf16[256,512]{1,0:T(8,128)(2,1)S(1)}, u32[]{:S(2)}, u32[]{:S(2)}) %collective-permute-start.8) | collective-permute-done | bytes 262176 | tf_op jit(solution)/shard_map/ppermute | solution.py:28
  32.3 3.3 %collective-permute-done.5 = bf16[256,512]{1,0:T(8,128)(2,1)S(1)} collective-permute-done((bf16[256,512]{1,0:T(8,128)(2,1)S(1)}, bf16[256,512]{1,0:T(8,128)(2,1)S(1)}, u32[]{:S(2)}, u32[]{:S(2)}) %collective-permute-start.5) | collective-permute-done | bytes 262176 | tf_op jit(solution)/shard_map/ppermute | solution.py:28
  37.4 2.3 %collective-permute-done.12 = bf16[256,512]{1,0:T(8,128)(2,1)S(1)} collective-permute-done((bf16[256,512]{1,0:T(8,128)(2,1)S(1)}, bf16[256,512]{1,0:T(8,128)(2,1)S(1)}, u32[]{:S(2)}, u32[]{:S(2)}) %collective-permute-start.12) | collective-permute-done | bytes 262176 | tf_op jit(solution)/shard_map/ppermute | solution.py:28
  41.5 2.9 %collective-permute-done.10 = bf16[256,512]{1,0:T(8,128)(2,1)S(1)} collective-permute-done((bf16[256,512]{1,0:T(8,128)(2,1)S(1)}, bf16[256,512]{1,0:T(8,128)(2,1)S(1)}, u32[]{:S(2)}, u32[]{:S(2)}) %collective-permute-start.10) | collective-permute-done | bytes 262176 | tf_op jit(solution)/shard_map/ppermute | solution.py:25
  45.7 2.1 %fusion.80 = f32[256,1792]{1,0:T(8,128)S(1)} fusion(bf16[256,2048]{1,0:T(8,128)(2,1)S(1)} %get-tuple-element.155, bf16[2048,1792]{1,0:T(8,128)(2,1)S(1)} %copy-done.2), kind=kOutput, calls=%fused_computation.116 | convolution fusion | flops 1879048192 | bytes 10223616 | tf_op jit(solution)/shard_map/dot_general | solution.py:49
  48.8 2.1 %fusion.81 = f32[256,1792]{1,0:T(8,128)S(1)} fusion(bf16[256,2048]{1,0:T(8,128)(2,1)S(1)} %get-tuple-element.155, bf16[2048,1792]{1,0:T(8,128)(2,1)S(1)} %bitcast.30), kind=kOutput, calls=%fused_computation.117 | convolution fusion | flops 1879048192 | bytes 10223616 | tf_op jit(solution)/shard_map/dot_general | solution.py:49
  53.9 2.1 %convolution_convert_fusion.4 = bf16[256,1792]{1,0:T(8,128)(2,1)S(1)} fusion(bf16[256,2048]{1,0:T(8,128)(2,1)S(1)} %constant_dynamic-update-slice_fusion.10, bf16[2048,1792]{1,0:T(8,128)(2,1)S(1)} %bitcast.30), kind=kOutput, calls=%fused_computation.4 | convolution fusion | flops 1879506944 | bytes 9306112 | tf_op jit(solution)/shard_map/dot_general | solution.py:49
  55.9 2.1 %convolution_convert_fusion.5 = bf16[256,1792]{1,0:T(8,128)(2,1)S(1)} fusion(bf16[256,2048]{1,0:T(8,128)(2,1)S(1)} %constant_dynamic-update-slice_fusion.10, bf16[2048,1792]{1,0:T(8,128)(2,1)S(1)} %copy-done.2), kind=kOutput, calls=%fused_computation.5 | convolution fusion | flops 1879506944 | bytes 9306112 | tf_op jit(solution)/shard_map/dot_general | solution.py:49
  58.7 2.1 %convolution_convert_fusion.3 = bf16[256,1792]{1,0:T(8,128)(2,1)S(1)} fusion(bf16[256,2048]{1,0:T(8,128)(2,1)S(1)} %constant_dynamic-update-slice_fusion.6, bf16[1792,2048]{1,0:T(8,128)(2,1)S(1)} %bitcast.28), kind=kOutput, calls=%fused_computation.3 | convolution fusion | flops 1879506944 | bytes 9306112 | tf_op jit(solution)/shard_map/dot_general | solution.py:49
  61.0 2.1 %fusion.82 = f32[256,1792]{1,0:T(8,128)S(1)} fusion(bf16[256,2048]{1,0:T(8,128)(2,1)S(1)} %get-tuple-element.104, bf16[1792,2048]{1,0:T(8,128)(2,1)S(1)} %bitcast.28), kind=kOutput, calls=%fused_computation.118 | convolution fusion | flops 1879048192 | bytes 10223616 | tf_op jit(solution)/shard_map/dot_general | solution.py:49
  92.0 2.0 %collective-permute-done.37 = bf16[256,512]{1,0:T(8,128)(2,1)S(1)} collective-permute-done((bf16[256,512]{1,0:T(8,128)(2,1)S(1)}, bf16[256,512]{1,0:T(8,128)(2,1)S(1)}, u32[]{:S(2)}, u32[]{:S(2)}) %collective-permute-start.37) | collective-permute-done | bytes 262176 | tf_op jit(solution)/shard_map/ppermute | solution.py:25
  94.1 1.8 %collective-permute-start.40 = (bf16[256,512]{1,0:T(8,128)(2,1)S(1)}, bf16[256,512]{1,0:T(8,128)(2,1)S(1)}, u32[]{:S(2)}, u32[]{:S(2)}) collective-permute-start(bf16[256,512]{1,0:T(8,128)(2,1)S(1)} %get-tuple-element.126), channel_id=1, source_target_pairs={{4,0},{8,4},{12,8},{14,12},{10,14},{6,10},{2,6},{0,2},{5,1},{9,5},... | collective-permute-start | bytes 786440 | tf_op jit(solution)/shard_map/ppermute | solution.py:28
  96.2 6.0 %convolution_convert_fusion.2 = bf16[1792,2048]{1,0:T(8,128)(2,1)} fusion(bf16[512,1792]{1,0:T(8,128)(2,1)S(1)} %constant_dynamic-update-slice_fusion, bf16[256,2048]{1,0:T(8,128)(2,1)S(1)} %constant_dynamic-update-slice_fusion.6, bf16[256,2048]{1,0:T(8,128)(2,1)S(1)} %get-tuple-element.104), kind=kOutput, calls=%fused_computation.2 | convolution fusion | flops 3765960704 | bytes 11272192 | tf_op jit(solution)/shard_map/dot_general | solution.py:49
  106.4 6.1 %convolution_convert_fusion.1 = bf16[2048,1792]{1,0:T(8,128)(2,1)} fusion(bf16[512,1792]{1,0:T(8,128)(2,1)S(1)} %constant_dynamic-update-slice_fusion.2, bf16[256,2048]{1,0:T(8,128)(2,1)S(1)} %constant_dynamic-update-slice_fusion.10, bf16[256,2048]{1,0:T(8,128)(2,1)S(1)} %get-tuple-element.155), kind=kOutput, calls=%fused_computation.1 | convolution fusion | flops 3765960704 | bytes 11272192 | tf_op jit(solution)/shard_map/dot_general | solution.py:49
  116.6 6.1 %convolution_convert_fusion = bf16[2048,1792]{1,0:T(8,128)(2,1)} fusion(bf16[512,1792]{1,0:T(8,128)(2,1)S(1)} %constant_dynamic-update-slice_fusion.4, bf16[256,2048]{1,0:T(8,128)(2,1)S(1)} %constant_dynamic-update-slice_fusion.10, bf16[256,2048]{1,0:T(8,128)(2,1)S(1)} %get-tuple-element.155), kind=kOutput, calls=%fused_computation | convolution fusion | flops 3765960704 | bytes 11272192 | tf_op jit(solution)/shard_map/dot_general | solution.py:49
  124.3 2.9 %collective-permute-done.48 = bf16[256,512]{1,0:T(8,128)(2,1)S(1)} collective-permute-done((bf16[256,512]{1,0:T(8,128)(2,1)S(1)}, bf16[256,512]{1,0:T(8,128)(2,1)S(1)}, u32[]{:S(2)}, u32[]{:S(2)}) %collective-permute-start.48) | collective-permute-done | bytes 262176 | tf_op jit(solution)/shard_map/ppermute | solution.py:25
  (177 shorter events, 55.1 us)
Async XLA Ops:
  0.6 10.4 %collective-permute-start = (bf16[256,512]{1,0:T(8,128)(2,1)}, bf16[256,512]{1,0:T(8,128)(2,1)S(1)}, u32[]{:S(2)}, u32[]{:S(2)}) collective-permute-start(bf16[256,512]{1,0:T(8,128)(2,1)} %param.5), channel_id=1, source_target_pairs={{0,4},{4,8},{8,12},{12,14},{14,10},{10,6},{6,2},{2,0},{1,5},{5,9},... | collective-permute-start | bytes 786440 | tf_op jit(solution)/shard_map/ppermute | solution.py:25
  3.7 9.4 %collective-permute-start.1 = (bf16[256,512]{1,0:T(8,128)(2,1)}, bf16[256,512]{1,0:T(8,128)(2,1)S(1)}, u32[]{:S(2)}, u32[]{:S(2)}) collective-permute-start(bf16[256,512]{1,0:T(8,128)(2,1)} %param.5), channel_id=1, source_target_pairs={{4,0},{8,4},{12,8},{14,12},{10,14},{6,10},{2,6},{0,2},{5,1},{9,5},... | collective-permute-start | bytes 786440 | tf_op jit(solution)/shard_map/ppermute | solution.py:28
  3.7 12.9 %collective-permute-start.6 = (bf16[256,512]{1,0:T(8,128)(2,1)}, bf16[256,512]{1,0:T(8,128)(2,1)S(1)}, u32[]{:S(2)}, u32[]{:S(2)}) collective-permute-start(bf16[256,512]{1,0:T(8,128)(2,1)} %param.9), channel_id=1, source_target_pairs={{0,4},{4,8},{8,12},{12,14},{14,10},{10,6},{6,2},{2,0},{1,5},{5,9},... | collective-permute-start | bytes 786440 | tf_op jit(solution)/shard_map/ppermute | solution.py:25
  5.7 13.0 %collective-permute-start.7 = (bf16[256,512]{1,0:T(8,128)(2,1)}, bf16[256,512]{1,0:T(8,128)(2,1)S(1)}, u32[]{:S(2)}, u32[]{:S(2)}) collective-permute-start(bf16[256,512]{1,0:T(8,128)(2,1)} %param.9), channel_id=1, source_target_pairs={{4,0},{8,4},{12,8},{14,12},{10,14},{6,10},{2,6},{0,2},{5,1},{9,5},... | collective-permute-start | bytes 786440 | tf_op jit(solution)/shard_map/ppermute | solution.py:28
  13.1 11.2 %collective-permute-start.2 = (bf16[256,512]{1,0:T(8,128)(2,1)S(1)}, bf16[256,512]{1,0:T(8,128)(2,1)S(1)}, u32[]{:S(2)}, u32[]{:S(2)}) collective-permute-start(bf16[256,512]{1,0:T(8,128)(2,1)S(1)} %collective-permute-done.1), channel_id=1, source_target_pairs={{4,0},{8,4},{12,8},{14,12},{10,14},{6,10},{2,6},{0,2},{5,1},{9,5},... | collective-permute-start | bytes 786440 | tf_op jit(solution)/shard_map/ppermute | solution.py:28
  13.2 11.2 %collective-permute-start.3 = (bf16[256,512]{1,0:T(8,128)(2,1)S(1)}, bf16[256,512]{1,0:T(8,128)(2,1)S(1)}, u32[]{:S(2)}, u32[]{:S(2)}) collective-permute-start(bf16[256,512]{1,0:T(8,128)(2,1)S(1)} %collective-permute-done), channel_id=1, source_target_pairs={{0,4},{4,8},{8,12},{12,14},{14,10},{10,6},{6,2},{2,0},{1,5},{5,9},... | collective-permute-start | bytes 786440 | tf_op jit(solution)/shard_map/ppermute | solution.py:25
  18.8 11.2 %collective-permute-start.8 = (bf16[256,512]{1,0:T(8,128)(2,1)S(1)}, bf16[256,512]{1,0:T(8,128)(2,1)S(1)}, u32[]{:S(2)}, u32[]{:S(2)}) collective-permute-start(bf16[256,512]{1,0:T(8,128)(2,1)S(1)} %collective-permute-done.7), channel_id=1, source_target_pairs={{4,0},{8,4},{12,8},{14,12},{10,14},{6,10},{2,6},{0,2},{5,1},{9,5},... | collective-permute-start | bytes 786440 | tf_op jit(solution)/shard_map/ppermute | solution.py:28
  18.8 11.2 %collective-permute-start.9 = (bf16[256,512]{1,0:T(8,128)(2,1)S(1)}, bf16[256,512]{1,0:T(8,128)(2,1)S(1)}, u32[]{:S(2)}, u32[]{:S(2)}) collective-permute-start(bf16[256,512]{1,0:T(8,128)(2,1)S(1)} %collective-permute-done.6), channel_id=1, source_target_pairs={{0,4},{4,8},{8,12},{12,14},{14,10},{10,6},{6,2},{2,0},{1,5},{5,9},... | collective-permute-start | bytes 786440 | tf_op jit(solution)/shard_map/ppermute | solution.py:25
  24.4 11.2 %collective-permute-start.4 = (bf16[256,512]{1,0:T(8,128)(2,1)S(1)}, bf16[256,512]{1,0:T(8,128)(2,1)S(1)}, u32[]{:S(2)}, u32[]{:S(2)}) collective-permute-start(bf16[256,512]{1,0:T(8,128)(2,1)S(1)} %collective-permute-done.3), channel_id=1, source_target_pairs={{0,4},{4,8},{8,12},{12,14},{14,10},{10,6},{6,2},{2,0},{1,5},{5,9},... | collective-permute-start | bytes 786440 | tf_op jit(solution)/shard_map/ppermute | solution.py:25
  26.0 9.7 %collective-permute-start.5 = (bf16[256,512]{1,0:T(8,128)(2,1)S(1)}, bf16[256,512]{1,0:T(8,128)(2,1)S(1)}, u32[]{:S(2)}, u32[]{:S(2)}) collective-permute-start(bf16[256,512]{1,0:T(8,128)(2,1)S(1)} %collective-permute-done.2), channel_id=1, source_target_pairs={{4,0},{8,4},{12,8},{14,12},{10,14},{6,10},{2,6},{0,2},{5,1},{9,5},... | collective-permute-start | bytes 786440 | tf_op jit(solution)/shard_map/ppermute | solution.py:28
  26.6 13.9 %collective-permute-start.13 = (bf16[256,512]{1,0:T(8,128)(2,1)S(1)}, bf16[256,512]{1,0:T(8,128)(2,1)S(1)}, u32[]{:S(2)}, u32[]{:S(2)}) collective-permute-start(bf16[256,512]{1,0:T(8,128)(2,1)S(1)} %get-tuple-element.160), channel_id=1, source_target_pairs={{0,1},{1,0},{2,3},{3,2},{4,5},{5,4},{6,7},{7,6},{8,9},{9,8},{10,11... | collective-permute-start | bytes 786440 | tf_op jit(solution)/shard_map/ppermute | solution.py:41
  30.0 9.8 %collective-permute-start.11 = (bf16[256,512]{1,0:T(8,128)(2,1)S(1)}, bf16[256,512]{1,0:T(8,128)(2,1)S(1)}, u32[]{:S(2)}, u32[]{:S(2)}) collective-permute-start(bf16[256,512]{1,0:T(8,128)(2,1)S(1)} %collective-permute-done.9), channel_id=1, source_target_pairs={{0,4},{4,8},{8,12},{12,14},{14,10},{10,6},{6,2},{2,0},{1,5},{5,9},... | collective-permute-start | bytes 786440 | tf_op jit(solution)/shard_map/ppermute | solution.py:25
  39.8 13.2 %collective-permute-start.15 = (bf16[256,512]{1,0:T(8,128)(2,1)S(1)}, bf16[256,512]{1,0:T(8,128)(2,1)S(1)}, u32[]{:S(2)}, u32[]{:S(2)}) collective-permute-start(bf16[256,512]{1,0:T(8,128)(2,1)S(1)} %get-tuple-element.156), channel_id=1, source_target_pairs={{0,1},{1,0},{2,3},{3,2},{4,5},{5,4},{6,7},{7,6},{8,9},{9,8},{10,11... | collective-permute-start | bytes 786440 | tf_op jit(solution)/shard_map/ppermute | solution.py:41
  39.8 12.6 %collective-permute-start.14 = (bf16[256,512]{1,0:T(8,128)(2,1)S(1)}, bf16[256,512]{1,0:T(8,128)(2,1)S(1)}, u32[]{:S(2)}, u32[]{:S(2)}) collective-permute-start(bf16[256,512]{1,0:T(8,128)(2,1)S(1)} %get-tuple-element.158), channel_id=1, source_target_pairs={{0,1},{1,0},{2,3},{3,2},{4,5},{5,4},{6,7},{7,6},{8,9},{9,8},{10,11... | collective-permute-start | bytes 786440 | tf_op jit(solution)/shard_map/ppermute | solution.py:41
  40.5 12.6 %collective-permute-start.24 = (bf16[256,512]{1,0:T(8,128)(2,1)S(1)}, bf16[256,512]{1,0:T(8,128)(2,1)S(1)}, u32[]{:S(2)}, u32[]{:S(2)}) collective-permute-start(bf16[256,512]{1,0:T(8,128)(2,1)S(1)} %get-tuple-element.149), channel_id=1, source_target_pairs={{0,1},{1,0},{2,3},{3,2},{4,5},{5,4},{6,7},{7,6},{8,9},{9,8},{10,11... | collective-permute-start | bytes 786440 | tf_op jit(solution)/shard_map/ppermute | solution.py:41
  40.8 12.3 %collective-permute-start.23 = (bf16[256,512]{1,0:T(8,128)(2,1)S(1)}, bf16[256,512]{1,0:T(8,128)(2,1)S(1)}, u32[]{:S(2)}, u32[]{:S(2)}) collective-permute-start(bf16[256,512]{1,0:T(8,128)(2,1)S(1)} %get-tuple-element.151), channel_id=1, source_target_pairs={{0,1},{1,0},{2,3},{3,2},{4,5},{5,4},{6,7},{7,6},{8,9},{9,8},{10,11... | collective-permute-start | bytes 786440 | tf_op jit(solution)/shard_map/ppermute | solution.py:41
  84.1 9.9 %collective-permute-start.38 = (bf16[256,512]{1,0:T(8,128)(2,1)S(1)}, bf16[256,512]{1,0:T(8,128)(2,1)S(1)}, u32[]{:S(2)}, u32[]{:S(2)}) collective-permute-start(bf16[256,512]{1,0:T(8,128)(2,1)S(1)} %broadcast_select_fusion.3), channel_id=1, source_target_pairs={{4,0},{8,4},{12,8},{14,12},{10,14},{6,10},{2,6},{0,2},{5,1},{9,5},... | collective-permute-start | bytes 786440 | tf_op jit(solution)/shard_map/ppermute | solution.py:28
  86.3 15.9 %collective-permute-start.45 = (bf16[256,512]{1,0:T(8,128)(2,1)S(1)}, bf16[256,512]{1,0:T(8,128)(2,1)S(1)}, u32[]{:S(2)}, u32[]{:S(2)}) collective-permute-start(bf16[256,512]{1,0:T(8,128)(2,1)S(1)} %select_add_fusion.7), channel_id=1, source_target_pairs={{4,0},{8,4},{12,8},{14,12},{10,14},{6,10},{2,6},{0,2},{5,1},{9,5},... | collective-permute-start | bytes 786440 | tf_op jit(solution)/shard_map/ppermute | solution.py:28
  87.0 15.2 %collective-permute-start.44 = (bf16[256,512]{1,0:T(8,128)(2,1)S(1)}, bf16[256,512]{1,0:T(8,128)(2,1)S(1)}, u32[]{:S(2)}, u32[]{:S(2)}) collective-permute-start(bf16[256,512]{1,0:T(8,128)(2,1)S(1)} %broadcast_select_fusion), channel_id=1, source_target_pairs={{0,4},{4,8},{8,12},{12,14},{14,10},{10,6},{6,2},{2,0},{1,5},{5,9},... | collective-permute-start | bytes 786440 | tf_op jit(solution)/shard_map/ppermute | solution.py:25
  94.1 10.4 %collective-permute-start.40 = (bf16[256,512]{1,0:T(8,128)(2,1)S(1)}, bf16[256,512]{1,0:T(8,128)(2,1)S(1)}, u32[]{:S(2)}, u32[]{:S(2)}) collective-permute-start(bf16[256,512]{1,0:T(8,128)(2,1)S(1)} %get-tuple-element.126), channel_id=1, source_target_pairs={{4,0},{8,4},{12,8},{14,12},{10,14},{6,10},{2,6},{0,2},{5,1},{9,5},... | collective-permute-start | bytes 786440 | tf_op jit(solution)/shard_map/ppermute | solution.py:28
  102.3 10.1 %collective-permute-start.46 = (bf16[256,512]{1,0:T(8,128)(2,1)S(1)}, bf16[256,512]{1,0:T(8,128)(2,1)S(1)}, u32[]{:S(2)}, u32[]{:S(2)}) collective-permute-start(bf16[256,512]{1,0:T(8,128)(2,1)S(1)} %get-tuple-element.131), channel_id=1, source_target_pairs={{0,4},{4,8},{8,12},{12,14},{14,10},{10,6},{6,2},{2,0},{1,5},{5,9},... | collective-permute-start | bytes 786440 | tf_op jit(solution)/shard_map/ppermute | solution.py:25
  104.6 18.8 %collective-permute-start.42 = (bf16[256,512]{1,0:T(8,128)(2,1)S(1)}, bf16[256,512]{1,0:T(8,128)(2,1)S(1)}, u32[]{:S(2)}, u32[]{:S(2)}) collective-permute-start(bf16[256,512]{1,0:T(8,128)(2,1)S(1)} %select_add_fusion.4), channel_id=1, source_target_pairs={{4,0},{8,4},{12,8},{14,12},{10,14},{6,10},{2,6},{0,2},{5,1},{9,5},... | collective-permute-start | bytes 786440 | tf_op jit(solution)/shard_map/ppermute | solution.py:28
  113.0 14.2 %collective-permute-start.49 = (bf16[256,512]{1,0:T(8,128)(2,1)S(1)}, bf16[256,512]{1,0:T(8,128)(2,1)S(1)}, u32[]{:S(2)}, u32[]{:S(2)}) collective-permute-start(bf16[256,512]{1,0:T(8,128)(2,1)S(1)} %select_add_fusion), channel_id=1, source_target_pairs={{4,0},{8,4},{12,8},{14,12},{10,14},{6,10},{2,6},{0,2},{5,1},{9,5},... | collective-permute-start | bytes 786440 | tf_op jit(solution)/shard_map/ppermute | solution.py:28
  115.0 12.1 %collective-permute-start.48 = (bf16[256,512]{1,0:T(8,128)(2,1)S(1)}, bf16[256,512]{1,0:T(8,128)(2,1)S(1)}, u32[]{:S(2)}, u32[]{:S(2)}) collective-permute-start(bf16[256,512]{1,0:T(8,128)(2,1)S(1)} %select_add_fusion.3), channel_id=1, source_target_pairs={{0,4},{4,8},{8,12},{12,14},{14,10},{10,6},{6,2},{2,0},{1,5},{5,9},... | collective-permute-start | bytes 786440 | tf_op jit(solution)/shard_map/ppermute | solution.py:25
  (39 other events, 208.2 us)

commit v3 on v2

--- a/solution.py
+++ b/solution.py
@@ -151,24 +151,25 @@
         done = g.swap(step - 1, mark)
     t.swap(m, done)
     gate_own, up_own = dot(t.own, gate_weight, 1, 0), dot(t.own, up_weight, 1, 0)
-    t_got = after(t.got, (gate_own, up_own))
-    gate_other, up_other = dot(t_got, gate_weight, 1, 0).astype(BF16), dot(t_got, up_weight, 1, 0).astype(BF16)
+    gate_other, up_other = dot(t.got, gate_weight, 1, 0).astype(BF16), dot(t.got, up_weight, 1, 0).astype(BF16)
     gate_got, up_got = swap_cores(gate_other), swap_cores(up_other)
     g.swap(m, gate_own)
     g_own, g_got = after((g.own, g.got), (gate_other, up_other))
     grad_other = dot(g_got, down_weight, 1, 1).astype(BF16)
+    grad_own = dot(g_own, down_weight, 1, 1)
     grad_got = swap_cores(grad_other)
-    grad_own = dot(g_own, down_weight, 1, 1)
 
     gate_value, up_value = gate_own + gate_got.astype(F32), up_own + up_got.astype(F32)
     sigmoid_gate = jax.nn.sigmoid(gate_value)
     activated = gate_value * sigmoid_gate
     slope = up_value * sigmoid_gate * (1.0 + gate_value * (1.0 - sigmoid_gate))
     hidden = (activated * up_value).astype(BF16)
+    activated, slope = activated.astype(BF16), slope.astype(BF16)
     activated, slope, hidden = lax.optimization_barrier((activated, slope, hidden))
     hidden_got = swap_cores(hidden)
     hidden_grad = after(grad_own, hidden) + grad_got.astype(F32)
-    gate_grad, up_grad = (hidden_grad * slope).astype(BF16), (hidden_grad * activated).astype(BF16)
+    gate_grad = (hidden_grad * slope.astype(F32)).astype(BF16)
+    up_grad = (hidden_grad * activated.astype(F32)).astype(BF16)
     gate_grad, up_grad = lax.optimization_barrier((gate_grad, up_grad))
     gate_grad_got, up_grad_got = swap_cores(gate_grad), swap_cores(up_grad)
     hidden_both = jnp.concatenate([hidden, hidden_got], 0)
@@ -199,23 +200,22 @@
         return [wgrads[-1]]
 
     o, i = Terms(ring, output_term), Terms(ring, input_term)
+    o_sum, i_sum = Sum(ring, o, True), Sum(ring, i, False)
     o.work_out([m], [])
     i.work_out([m], o.made[m][1])
-    o_sum, i_sum = Sum(ring, o, True), Sum(ring, i, False)
     mark = o_sum.advance([])
     done = o.work_out([m - 1, 1], (mark, i.made[m][1]))
     mark = i_sum.advance(done)
     done = i.work_out([m - 1], mark)
     for distance in range(m - 1, 0, -1):
         mark = o_sum.advance(done)
-        done = i.work_out([m - distance], mark)
+        done = i.work_out([m - distance, distance], mark)
         if distance <= 2:
             done += wgrad_work(mark)
         mark = i_sum.advance(done)
         pairs = [distance - 1, m - distance + 1]
         done = o.work_out(pairs, mark) + i.work_out(pairs[:1], mark)
-        if distance == 1:
-            wgrad_work(mark)
+    wgrad_work((mark, o_sum.ahead))
     output, input_grad = o_sum.total(), i_sum.total()
     return output.astype(BF16), input_grad.astype(BF16), wgrads[1], wgrads[2], wgrads[0]
 

time: 128 us -> 124 us (0.969)
  waiting for transfers between devices: 37.3 us -> 35.3 us
    ppermute x14, waiting for transfers between devices: 16.3 us -> 14.5 us  [up(): return lax.ppermute(value, 'tp', self.up_hops)]
  transfers between devices with their start and end apart: 50 -> 50, of which waited for: 19 -> 18; matrix products, arithmetic and copies ran while one was open for 39% -> 40% of each run, Pallas kernels for 0% -> 0%
where the time goes in v3:
time: 124 us
  matrix products  44.4 us (36%)
  starting transfers between devices  36 us (29%)
  waiting for transfers between devices  35.3 us (28%)
  other arithmetic  4.82 us (4%)
  local copies, waits for them, and re-layouts  2.22 us (2%)
  between operations  1.41 us (1%)
    dot_general x21, matrix products, dot(): lax.dot_general(left, right, (((left_dim,), (right_dim,)), ((), ())), pre...  44.4 us
    ppermute x14, starting transfers between devices, up(): return lax.ppermute(value, 'tp', self.up_hops)  21.8 us
    ppermute x14, waiting for transfers between devices, down(): return lax.ppermute(value, 'tp', self.down_hops)  18.4 us
    ppermute x14, waiting for transfers between devices, up(): return lax.ppermute(value, 'tp', self.up_hops)  14.5 us
    ppermute x14, starting transfers between devices, down(): return lax.ppermute(value, 'tp', self.down_hops)  8.84 us
    ppermute x22, starting transfers between devices, swap_cores(): return lax.ppermute(value, 'dp', [(0, 1), (1, 0)])  5.34 us
  transfers between devices with their start and end apart: 50, of which 18 were waited for; matrix products, arithmetic and copies ran while one was open for 40% of the time, Pallas kernels for 0%

profile of v3, /device:TPU:0, one launch (start us, length us, event | category | flops | bytes accessed | tf_op | source)
XLA Modules:
  0.0 124.1 jit_solution(16929621072488145148)
XLA Ops:
  0.6 3.1 %collective-permute-start = (bf16[256,512]{1,0:T(8,128)(2,1)}, bf16[256,512]{1,0:T(8,128)(2,1)S(1)}, u32[]{:S(2)}, u32[]{:S(2)}) collective-permute-start(bf16[256,512]{1,0:T(8,128)(2,1)} %param.5), channel_id=1, source_target_pairs={{0,4},{4,8},{8,12},{12,14},{14,10},{10,6},{6,2},{2,0},{1,5},{5,9},... | collective-permute-start | bytes 786440 | tf_op jit(solution)/shard_map/ppermute | solution.py:25
  3.7 2.0 %collective-permute-start.6 = (bf16[256,512]{1,0:T(8,128)(2,1)}, bf16[256,512]{1,0:T(8,128)(2,1)S(1)}, u32[]{:S(2)}, u32[]{:S(2)}) collective-permute-start(bf16[256,512]{1,0:T(8,128)(2,1)} %param.9), channel_id=1, source_target_pairs={{0,4},{4,8},{8,12},{12,14},{14,10},{10,6},{6,2},{2,0},{1,5},{5,9},... | collective-permute-start | bytes 786440 | tf_op jit(solution)/shard_map/ppermute | solution.py:25
  5.7 5.3 %collective-permute-done = bf16[256,512]{1,0:T(8,128)(2,1)S(1)} collective-permute-done((bf16[256,512]{1,0:T(8,128)(2,1)}, bf16[256,512]{1,0:T(8,128)(2,1)S(1)}, u32[]{:S(2)}, u32[]{:S(2)}) %collective-permute-start) | collective-permute-done | bytes 262176 | tf_op jit(solution)/shard_map/ppermute | solution.py:25
  11.0 2.2 %collective-permute-done.1 = bf16[256,512]{1,0:T(8,128)(2,1)S(1)} collective-permute-done((bf16[256,512]{1,0:T(8,128)(2,1)}, bf16[256,512]{1,0:T(8,128)(2,1)S(1)}, u32[]{:S(2)}, u32[]{:S(2)}) %collective-permute-start.1) | collective-permute-done | bytes 262176 | tf_op jit(solution)/shard_map/ppermute | solution.py:28
  13.2 2.0 %collective-permute-start.3 = (bf16[256,512]{1,0:T(8,128)(2,1)S(1)}, bf16[256,512]{1,0:T(8,128)(2,1)S(1)}, u32[]{:S(2)}, u32[]{:S(2)}) collective-permute-start(bf16[256,512]{1,0:T(8,128)(2,1)S(1)} %collective-permute-done), channel_id=1, source_target_pairs={{0,4},{4,8},{8,12},{12,14},{14,10},{10,6},{6,2},{2,0},{1,5},{5,9},... | collective-permute-start | bytes 786440 | tf_op jit(solution)/shard_map/ppermute | solution.py:25
  16.6 2.2 %collective-permute-done.7 = bf16[256,512]{1,0:T(8,128)(2,1)S(1)} collective-permute-done((bf16[256,512]{1,0:T(8,128)(2,1)}, bf16[256,512]{1,0:T(8,128)(2,1)S(1)}, u32[]{:S(2)}, u32[]{:S(2)}) %collective-permute-start.7) | collective-permute-done | bytes 262176 | tf_op jit(solution)/shard_map/ppermute | solution.py:28
  18.8 2.0 %collective-permute-start.9 = (bf16[256,512]{1,0:T(8,128)(2,1)S(1)}, bf16[256,512]{1,0:T(8,128)(2,1)S(1)}, u32[]{:S(2)}, u32[]{:S(2)}) collective-permute-start(bf16[256,512]{1,0:T(8,128)(2,1)S(1)} %collective-permute-done.6), channel_id=1, source_target_pairs={{0,4},{4,8},{8,12},{12,14},{14,10},{10,6},{6,2},{2,0},{1,5},{5,9},... | collective-permute-start | bytes 786440 | tf_op jit(solution)/shard_map/ppermute | solution.py:25
  20.8 3.6 %collective-permute-done.2 = bf16[256,512]{1,0:T(8,128)(2,1)S(1)} collective-permute-done((bf16[256,512]{1,0:T(8,128)(2,1)S(1)}, bf16[256,512]{1,0:T(8,128)(2,1)S(1)}, u32[]{:S(2)}, u32[]{:S(2)}) %collective-permute-start.2) | collective-permute-done | bytes 262176 | tf_op jit(solution)/shard_map/ppermute | solution.py:28
  26.7 3.3 %collective-permute-done.8 = bf16[256,512]{1,0:T(8,128)(2,1)S(1)} collective-permute-done((bf16[256,512]{1,0:T(8,128)(2,1)S(1)}, bf16[256,512]{1,0:T(8,128)(2,1)S(1)}, u32[]{:S(2)}, u32[]{:S(2)}) %collective-permute-start.8) | collective-permute-done | bytes 262176 | tf_op jit(solution)/shard_map/ppermute | solution.py:28
  32.3 3.3 %collective-permute-done.5 = bf16[256,512]{1,0:T(8,128)(2,1)S(1)} collective-permute-done((bf16[256,512]{1,0:T(8,128)(2,1)S(1)}, bf16[256,512]{1,0:T(8,128)(2,1)S(1)}, u32[]{:S(2)}, u32[]{:S(2)}) %collective-permute-start.5) | collective-permute-done | bytes 262176 | tf_op jit(solution)/shard_map/ppermute | solution.py:28
  37.4 2.3 %collective-permute-done.12 = bf16[256,512]{1,0:T(8,128)(2,1)S(1)} collective-permute-done((bf16[256,512]{1,0:T(8,128)(2,1)S(1)}, bf16[256,512]{1,0:T(8,128)(2,1)S(1)}, u32[]{:S(2)}, u32[]{:S(2)}) %collective-permute-start.12) | collective-permute-done | bytes 262176 | tf_op jit(solution)/shard_map/ppermute | solution.py:28
  41.5 2.9 %collective-permute-done.10 = bf16[256,512]{1,0:T(8,128)(2,1)S(1)} collective-permute-done((bf16[256,512]{1,0:T(8,128)(2,1)S(1)}, bf16[256,512]{1,0:T(8,128)(2,1)S(1)}, u32[]{:S(2)}, u32[]{:S(2)}) %collective-permute-start.10) | collective-permute-done | bytes 262176 | tf_op jit(solution)/shard_map/ppermute | solution.py:25
  45.8 2.1 %fusion.80 = f32[256,1792]{1,0:T(8,128)S(1)} fusion(bf16[256,2048]{1,0:T(8,128)(2,1)S(1)} %get-tuple-element.153, bf16[2048,1792]{1,0:T(8,128)(2,1)S(1)} %copy-done.2), kind=kOutput, calls=%fused_computation.117 | convolution fusion | flops 1879048192 | bytes 10223616 | tf_op jit(solution)/shard_map/dot_general | solution.py:49
  48.8 2.1 %fusion.81 = f32[256,1792]{1,0:T(8,128)S(1)} fusion(bf16[256,2048]{1,0:T(8,128)(2,1)S(1)} %get-tuple-element.153, bf16[2048,1792]{1,0:T(8,128)(2,1)S(1)} %bitcast.30), kind=kOutput, calls=%fused_computation.118 | convolution fusion | flops 1879048192 | bytes 10223616 | tf_op jit(solution)/shard_map/dot_general | solution.py:49
  53.9 2.1 %convolution_convert_fusion.4 = bf16[256,1792]{1,0:T(8,128)(2,1)S(1)} fusion(bf16[256,2048]{1,0:T(8,128)(2,1)S(1)} %constant_dynamic-update-slice_fusion.10, bf16[2048,1792]{1,0:T(8,128)(2,1)S(1)} %bitcast.30), kind=kOutput, calls=%fused_computation.4 | convolution fusion | flops 1879506944 | bytes 9306112 | tf_op jit(solution)/shard_map/dot_general | solution.py:49
  56.0 2.1 %convolution_convert_fusion.5 = bf16[256,1792]{1,0:T(8,128)(2,1)S(1)} fusion(bf16[256,2048]{1,0:T(8,128)(2,1)S(1)} %constant_dynamic-update-slice_fusion.10, bf16[2048,1792]{1,0:T(8,128)(2,1)S(1)} %copy-done.2), kind=kOutput, calls=%fused_computation.5 | convolution fusion | flops 1879506944 | bytes 9306112 | tf_op jit(solution)/shard_map/dot_general | solution.py:49
  58.7 2.1 %convolution_convert_fusion.3 = bf16[256,1792]{1,0:T(8,128)(2,1)S(1)} fusion(bf16[256,2048]{1,0:T(8,128)(2,1)S(1)} %constant_dynamic-update-slice_fusion.6, bf16[1792,2048]{1,0:T(8,128)(2,1)S(1)} %bitcast.28), kind=kOutput, calls=%fused_computation.3 | convolution fusion | flops 1879506944 | bytes 9306112 | tf_op jit(solution)/shard_map/dot_general | solution.py:49
  61.0 2.1 %fusion.82 = f32[256,1792]{1,0:T(8,128)S(1)} fusion(bf16[256,2048]{1,0:T(8,128)(2,1)S(1)} %get-tuple-element.102, bf16[1792,2048]{1,0:T(8,128)(2,1)S(1)} %bitcast.28), kind=kOutput, calls=%fused_computation.119 | convolution fusion | flops 1879048192 | bytes 10223616 | tf_op jit(solution)/shard_map/dot_general | solution.py:49
  91.2 2.0 %collective-permute-done.37 = bf16[256,512]{1,0:T(8,128)(2,1)S(1)} collective-permute-done((bf16[256,512]{1,0:T(8,128)(2,1)S(1)}, bf16[256,512]{1,0:T(8,128)(2,1)S(1)}, u32[]{:S(2)}, u32[]{:S(2)}) %collective-permute-start.37) | collective-permute-done | bytes 262176 | tf_op jit(solution)/shard_map/ppermute | solution.py:25
  93.3 1.8 %collective-permute-start.40 = (bf16[256,512]{1,0:T(8,128)(2,1)S(1)}, bf16[256,512]{1,0:T(8,128)(2,1)S(1)}, u32[]{:S(2)}, u32[]{:S(2)}) collective-permute-start(bf16[256,512]{1,0:T(8,128)(2,1)S(1)} %get-tuple-element.124), channel_id=1, source_target_pairs={{4,0},{8,4},{12,8},{14,12},{10,14},{6,10},{2,6},{0,2},{5,1},{9,5},... | collective-permute-start | bytes 786440 | tf_op jit(solution)/shard_map/ppermute | solution.py:28
  95.4 6.0 %convolution_convert_fusion.2 = bf16[1792,2048]{1,0:T(8,128)(2,1)} fusion(bf16[512,1792]{1,0:T(8,128)(2,1)S(1)} %constant_dynamic-update-slice_fusion, bf16[256,2048]{1,0:T(8,128)(2,1)S(1)} %constant_dynamic-update-slice_fusion.6, bf16[256,2048]{1,0:T(8,128)(2,1)S(1)} %get-tuple-element.102), kind=kOutput, calls=%fused_computation.2 | convolution fusion | flops 3765960704 | bytes 11272192 | tf_op jit(solution)/shard_map/dot_general | solution.py:49
  105.9 6.1 %convolution_convert_fusion.1 = bf16[2048,1792]{1,0:T(8,128)(2,1)} fusion(bf16[512,1792]{1,0:T(8,128)(2,1)S(1)} %constant_dynamic-update-slice_fusion.2, bf16[256,2048]{1,0:T(8,128)(2,1)S(1)} %constant_dynamic-update-slice_fusion.10, bf16[256,2048]{1,0:T(8,128)(2,1)S(1)} %get-tuple-element.153), kind=kOutput, calls=%fused_computation.1 | convolution fusion | flops 3765960704 | bytes 11272192 | tf_op jit(solution)/shard_map/dot_general | solution.py:49
  114.3 2.1 %collective-permute-done.41 = bf16[256,512]{1,0:T(8,128)(2,1)S(1)} collective-permute-done((bf16[256,512]{1,0:T(8,128)(2,1)S(1)}, bf16[256,512]{1,0:T(8,128)(2,1)S(1)}, u32[]{:S(2)}, u32[]{:S(2)}) %collective-permute-start.41) | collective-permute-done | bytes 262176 | tf_op jit(solution)/shard_map/ppermute | solution.py:25
  116.4 6.1 %convolution_convert_fusion = bf16[2048,1792]{1,0:T(8,128)(2,1)} fusion(bf16[512,1792]{1,0:T(8,128)(2,1)S(1)} %constant_dynamic-update-slice_fusion.4, bf16[256,2048]{1,0:T(8,128)(2,1)S(1)} %constant_dynamic-update-slice_fusion.10, bf16[256,2048]{1,0:T(8,128)(2,1)S(1)} %get-tuple-element.153), kind=kOutput, calls=%fused_computation | convolution fusion | flops 3765960704 | bytes 11272192 | tf_op jit(solution)/shard_map/dot_general | solution.py:49
  (172 shorter events, 52.0 us)
Async XLA Ops:
  0.6 10.4 %collective-permute-start = (bf16[256,512]{1,0:T(8,128)(2,1)}, bf16[256,512]{1,0:T(8,128)(2,1)S(1)}, u32[]{:S(2)}, u32[]{:S(2)}) collective-permute-start(bf16[256,512]{1,0:T(8,128)(2,1)} %param.5), channel_id=1, source_target_pairs={{0,4},{4,8},{8,12},{12,14},{14,10},{10,6},{6,2},{2,0},{1,5},{5,9},... | collective-permute-start | bytes 786440 | tf_op jit(solution)/shard_map/ppermute | solution.py:25
  3.7 12.9 %collective-permute-start.6 = (bf16[256,512]{1,0:T(8,128)(2,1)}, bf16[256,512]{1,0:T(8,128)(2,1)S(1)}, u32[]{:S(2)}, u32[]{:S(2)}) collective-permute-start(bf16[256,512]{1,0:T(8,128)(2,1)} %param.9), channel_id=1, source_target_pairs={{0,4},{4,8},{8,12},{12,14},{14,10},{10,6},{6,2},{2,0},{1,5},{5,9},... | collective-permute-start | bytes 786440 | tf_op jit(solution)/shard_map/ppermute | solution.py:25
  5.7 13.0 %collective-permute-start.7 = (bf16[256,512]{1,0:T(8,128)(2,1)}, bf16[256,512]{1,0:T(8,128)(2,1)S(1)}, u32[]{:S(2)}, u32[]{:S(2)}) collective-permute-start(bf16[256,512]{1,0:T(8,128)(2,1)} %param.9), channel_id=1, source_target_pairs={{4,0},{8,4},{12,8},{14,12},{10,14},{6,10},{2,6},{0,2},{5,1},{9,5},... | collective-permute-start | bytes 786440 | tf_op jit(solution)/shard_map/ppermute | solution.py:28
  13.1 11.2 %collective-permute-start.2 = (bf16[256,512]{1,0:T(8,128)(2,1)S(1)}, bf16[256,512]{1,0:T(8,128)(2,1)S(1)}, u32[]{:S(2)}, u32[]{:S(2)}) collective-permute-start(bf16[256,512]{1,0:T(8,128)(2,1)S(1)} %collective-permute-done.1), channel_id=1, source_target_pairs={{4,0},{8,4},{12,8},{14,12},{10,14},{6,10},{2,6},{0,2},{5,1},{9,5},... | collective-permute-start | bytes 786440 | tf_op jit(solution)/shard_map/ppermute | solution.py:28
  13.2 11.2 %collective-permute-start.3 = (bf16[256,512]{1,0:T(8,128)(2,1)S(1)}, bf16[256,512]{1,0:T(8,128)(2,1)S(1)}, u32[]{:S(2)}, u32[]{:S(2)}) collective-permute-start(bf16[256,512]{1,0:T(8,128)(2,1)S(1)} %collective-permute-done), channel_id=1, source_target_pairs={{0,4},{4,8},{8,12},{12,14},{14,10},{10,6},{6,2},{2,0},{1,5},{5,9},... | collective-permute-start | bytes 786440 | tf_op jit(solution)/shard_map/ppermute | solution.py:25
  18.8 11.2 %collective-permute-start.8 = (bf16[256,512]{1,0:T(8,128)(2,1)S(1)}, bf16[256,512]{1,0:T(8,128)(2,1)S(1)}, u32[]{:S(2)}, u32[]{:S(2)}) collective-permute-start(bf16[256,512]{1,0:T(8,128)(2,1)S(1)} %collective-permute-done.7), channel_id=1, source_target_pairs={{4,0},{8,4},{12,8},{14,12},{10,14},{6,10},{2,6},{0,2},{5,1},{9,5},... | collective-permute-start | bytes 786440 | tf_op jit(solution)/shard_map/ppermute | solution.py:28
  18.8 11.2 %collective-permute-start.9 = (bf16[256,512]{1,0:T(8,128)(2,1)S(1)}, bf16[256,512]{1,0:T(8,128)(2,1)S(1)}, u32[]{:S(2)}, u32[]{:S(2)}) collective-permute-start(bf16[256,512]{1,0:T(8,128)(2,1)S(1)} %collective-permute-done.6), channel_id=1, source_target_pairs={{0,4},{4,8},{8,12},{12,14},{14,10},{10,6},{6,2},{2,0},{1,5},{5,9},... | collective-permute-start | bytes 786440 | tf_op jit(solution)/shard_map/ppermute | solution.py:25
  24.4 11.2 %collective-permute-start.4 = (bf16[256,512]{1,0:T(8,128)(2,1)S(1)}, bf16[256,512]{1,0:T(8,128)(2,1)S(1)}, u32[]{:S(2)}, u32[]{:S(2)}) collective-permute-start(bf16[256,512]{1,0:T(8,128)(2,1)S(1)} %collective-permute-done.3), channel_id=1, source_target_pairs={{0,4},{4,8},{8,12},{12,14},{14,10},{10,6},{6,2},{2,0},{1,5},{5,9},... | collective-permute-start | bytes 786440 | tf_op jit(solution)/shard_map/ppermute | solution.py:25
  26.0 9.7 %collective-permute-start.5 = (bf16[256,512]{1,0:T(8,128)(2,1)S(1)}, bf16[256,512]{1,0:T(8,128)(2,1)S(1)}, u32[]{:S(2)}, u32[]{:S(2)}) collective-permute-start(bf16[256,512]{1,0:T(8,128)(2,1)S(1)} %collective-permute-done.2), channel_id=1, source_target_pairs={{4,0},{8,4},{12,8},{14,12},{10,14},{6,10},{2,6},{0,2},{5,1},{9,5},... | collective-permute-start | bytes 786440 | tf_op jit(solution)/shard_map/ppermute | solution.py:28
  26.6 13.9 %collective-permute-start.13 = (bf16[256,512]{1,0:T(8,128)(2,1)S(1)}, bf16[256,512]{1,0:T(8,128)(2,1)S(1)}, u32[]{:S(2)}, u32[]{:S(2)}) collective-permute-start(bf16[256,512]{1,0:T(8,128)(2,1)S(1)} %get-tuple-element.158), channel_id=1, source_target_pairs={{0,1},{1,0},{2,3},{3,2},{4,5},{5,4},{6,7},{7,6},{8,9},{9,8},{10,11... | collective-permute-start | bytes 786440 | tf_op jit(solution)/shard_map/ppermute | solution.py:41
  30.0 9.8 %collective-permute-start.11 = (bf16[256,512]{1,0:T(8,128)(2,1)S(1)}, bf16[256,512]{1,0:T(8,128)(2,1)S(1)}, u32[]{:S(2)}, u32[]{:S(2)}) collective-permute-start(bf16[256,512]{1,0:T(8,128)(2,1)S(1)} %collective-permute-done.9), channel_id=1, source_target_pairs={{0,4},{4,8},{8,12},{12,14},{14,10},{10,6},{6,2},{2,0},{1,5},{5,9},... | collective-permute-start | bytes 786440 | tf_op jit(solution)/shard_map/ppermute | solution.py:25
  39.8 13.2 %collective-permute-start.15 = (bf16[256,512]{1,0:T(8,128)(2,1)S(1)}, bf16[256,512]{1,0:T(8,128)(2,1)S(1)}, u32[]{:S(2)}, u32[]{:S(2)}) collective-permute-start(bf16[256,512]{1,0:T(8,128)(2,1)S(1)} %get-tuple-element.154), channel_id=1, source_target_pairs={{0,1},{1,0},{2,3},{3,2},{4,5},{5,4},{6,7},{7,6},{8,9},{9,8},{10,11... | collective-permute-start | bytes 786440 | tf_op jit(solution)/shard_map/ppermute | solution.py:41
  39.8 12.6 %collective-permute-start.14 = (bf16[256,512]{1,0:T(8,128)(2,1)S(1)}, bf16[256,512]{1,0:T(8,128)(2,1)S(1)}, u32[]{:S(2)}, u32[]{:S(2)}) collective-permute-start(bf16[256,512]{1,0:T(8,128)(2,1)S(1)} %get-tuple-element.156), channel_id=1, source_target_pairs={{0,1},{1,0},{2,3},{3,2},{4,5},{5,4},{6,7},{7,6},{8,9},{9,8},{10,11... | collective-permute-start | bytes 786440 | tf_op jit(solution)/shard_map/ppermute | solution.py:41
  40.5 12.6 %collective-permute-start.24 = (bf16[256,512]{1,0:T(8,128)(2,1)S(1)}, bf16[256,512]{1,0:T(8,128)(2,1)S(1)}, u32[]{:S(2)}, u32[]{:S(2)}) collective-permute-start(bf16[256,512]{1,0:T(8,128)(2,1)S(1)} %get-tuple-element.147), channel_id=1, source_target_pairs={{0,1},{1,0},{2,3},{3,2},{4,5},{5,4},{6,7},{7,6},{8,9},{9,8},{10,11... | collective-permute-start | bytes 786440 | tf_op jit(solution)/shard_map/ppermute | solution.py:41
  40.8 12.3 %collective-permute-start.23 = (bf16[256,512]{1,0:T(8,128)(2,1)S(1)}, bf16[256,512]{1,0:T(8,128)(2,1)S(1)}, u32[]{:S(2)}, u32[]{:S(2)}) collective-permute-start(bf16[256,512]{1,0:T(8,128)(2,1)S(1)} %get-tuple-element.149), channel_id=1, source_target_pairs={{0,1},{1,0},{2,3},{3,2},{4,5},{5,4},{6,7},{7,6},{8,9},{9,8},{10,11... | collective-permute-start | bytes 786440 | tf_op jit(solution)/shard_map/ppermute | solution.py:41
  83.4 9.9 %collective-permute-start.38 = (bf16[256,512]{1,0:T(8,128)(2,1)S(1)}, bf16[256,512]{1,0:T(8,128)(2,1)S(1)}, u32[]{:S(2)}, u32[]{:S(2)}) collective-permute-start(bf16[256,512]{1,0:T(8,128)(2,1)S(1)} %broadcast_select_fusion.3), channel_id=1, source_target_pairs={{4,0},{8,4},{12,8},{14,12},{10,14},{6,10},{2,6},{0,2},{5,1},{9,5},... | collective-permute-start | bytes 786440 | tf_op jit(solution)/shard_map/ppermute | solution.py:28
  85.5 15.9 %collective-permute-start.45 = (bf16[256,512]{1,0:T(8,128)(2,1)S(1)}, bf16[256,512]{1,0:T(8,128)(2,1)S(1)}, u32[]{:S(2)}, u32[]{:S(2)}) collective-permute-start(bf16[256,512]{1,0:T(8,128)(2,1)S(1)} %select_add_fusion.7), channel_id=1, source_target_pairs={{4,0},{8,4},{12,8},{14,12},{10,14},{6,10},{2,6},{0,2},{5,1},{9,5},... | collective-permute-start | bytes 786440 | tf_op jit(solution)/shard_map/ppermute | solution.py:28
  86.3 15.2 %collective-permute-start.44 = (bf16[256,512]{1,0:T(8,128)(2,1)S(1)}, bf16[256,512]{1,0:T(8,128)(2,1)S(1)}, u32[]{:S(2)}, u32[]{:S(2)}) collective-permute-start(bf16[256,512]{1,0:T(8,128)(2,1)S(1)} %broadcast_select_fusion), channel_id=1, source_target_pairs={{0,4},{4,8},{8,12},{12,14},{14,10},{10,6},{6,2},{2,0},{1,5},{5,9},... | collective-permute-start | bytes 786440 | tf_op jit(solution)/shard_map/ppermute | solution.py:25
  93.3 10.4 %collective-permute-start.40 = (bf16[256,512]{1,0:T(8,128)(2,1)S(1)}, bf16[256,512]{1,0:T(8,128)(2,1)S(1)}, u32[]{:S(2)}, u32[]{:S(2)}) collective-permute-start(bf16[256,512]{1,0:T(8,128)(2,1)S(1)} %get-tuple-element.124), channel_id=1, source_target_pairs={{4,0},{8,4},{12,8},{14,12},{10,14},{6,10},{2,6},{0,2},{5,1},{9,5},... | collective-permute-start | bytes 786440 | tf_op jit(solution)/shard_map/ppermute | solution.py:28
  101.5 10.4 %collective-permute-start.46 = (bf16[256,512]{1,0:T(8,128)(2,1)S(1)}, bf16[256,512]{1,0:T(8,128)(2,1)S(1)}, u32[]{:S(2)}, u32[]{:S(2)}) collective-permute-start(bf16[256,512]{1,0:T(8,128)(2,1)S(1)} %get-tuple-element.129), channel_id=1, source_target_pairs={{0,4},{4,8},{8,12},{12,14},{14,10},{10,6},{6,2},{2,0},{1,5},{5,9},... | collective-permute-start | bytes 786440 | tf_op jit(solution)/shard_map/ppermute | solution.py:25
  103.8 18.6 %collective-permute-start.42 = (bf16[256,512]{1,0:T(8,128)(2,1)S(1)}, bf16[256,512]{1,0:T(8,128)(2,1)S(1)}, u32[]{:S(2)}, u32[]{:S(2)}) collective-permute-start(bf16[256,512]{1,0:T(8,128)(2,1)S(1)} %select_add_fusion.4), channel_id=1, source_target_pairs={{4,0},{8,4},{12,8},{14,12},{10,14},{6,10},{2,6},{0,2},{5,1},{9,5},... | collective-permute-start | bytes 786440 | tf_op jit(solution)/shard_map/ppermute | solution.py:28
  105.6 10.8 %collective-permute-start.41 = (bf16[256,512]{1,0:T(8,128)(2,1)S(1)}, bf16[256,512]{1,0:T(8,128)(2,1)S(1)}, u32[]{:S(2)}, u32[]{:S(2)}) collective-permute-start(bf16[256,512]{1,0:T(8,128)(2,1)S(1)} %select_add_fusion.9), channel_id=1, source_target_pairs={{0,4},{4,8},{8,12},{12,14},{14,10},{10,6},{6,2},{2,0},{1,5},{5,9},... | collective-permute-start | bytes 786440 | tf_op jit(solution)/shard_map/ppermute | solution.py:25
  112.2 11.1 %collective-permute-start.48 = (bf16[256,512]{1,0:T(8,128)(2,1)S(1)}, bf16[256,512]{1,0:T(8,128)(2,1)S(1)}, u32[]{:S(2)}, u32[]{:S(2)}) collective-permute-start(bf16[256,512]{1,0:T(8,128)(2,1)S(1)} %select_add_fusion.3), channel_id=1, source_target_pairs={{0,4},{4,8},{8,12},{12,14},{14,10},{10,6},{6,2},{2,0},{1,5},{5,9},... | collective-permute-start | bytes 786440 | tf_op jit(solution)/shard_map/ppermute | solution.py:25
  113.8 9.5 %collective-permute-start.49 = (bf16[256,512]{1,0:T(8,128)(2,1)S(1)}, bf16[256,512]{1,0:T(8,128)(2,1)S(1)}, u32[]{:S(2)}, u32[]{:S(2)}) collective-permute-start(bf16[256,512]{1,0:T(8,128)(2,1)S(1)} %select_add_fusion), channel_id=1, source_target_pairs={{4,0},{8,4},{12,8},{14,12},{10,14},{6,10},{2,6},{0,2},{5,1},{9,5},... | collective-permute-start | bytes 786440 | tf_op jit(solution)/shard_map/ppermute | solution.py:28
  (37 other events, 202.7 us)

commit v4 on v3

--- a/solution.py
+++ b/solution.py
@@ -155,8 +155,8 @@
     gate_got, up_got = swap_cores(gate_other), swap_cores(up_other)
     g.swap(m, gate_own)
     g_own, g_got = after((g.own, g.got), (gate_other, up_other))
+    grad_own = dot(g_own, down_weight, 1, 1)
     grad_other = dot(g_got, down_weight, 1, 1).astype(BF16)
-    grad_own = dot(g_own, down_weight, 1, 1)
     grad_got = swap_cores(grad_other)
 
     gate_value, up_value = gate_own + gate_got.astype(F32), up_own + up_got.astype(F32)
@@ -214,7 +214,8 @@
             done += wgrad_work(mark)
         mark = i_sum.advance(done)
         pairs = [distance - 1, m - distance + 1]
-        done = o.work_out(pairs, mark) + i.work_out(pairs[:1], mark)
+        done = o.work_out(pairs, mark)
+        done += i.work_out(pairs[:1], (mark, done))
     wgrad_work((mark, o_sum.ahead))
     output, input_grad = o_sum.total(), i_sum.total()
     return output.astype(BF16), input_grad.astype(BF16), wgrads[1], wgrads[2], wgrads[0]

time: 124 us -> 124 us (level)
  no operation moved by 1% of the time
where the time goes in v4:
time: 124 us
  matrix products  44.4 us (36%)
  starting transfers between devices  36.1 us (29%)
  waiting for transfers between devices  35.2 us (28%)
  other arithmetic  4.82 us (4%)
  local copies, waits for them, and re-layouts  2.22 us (2%)
  between operations  1.41 us (1%)
    dot_general x21, matrix products, dot(): lax.dot_general(left, right, (((left_dim,), (right_dim,)), ((), ())), pre...  44.4 us
    ppermute x14, starting transfers between devices, up(): return lax.ppermute(value, 'tp', self.up_hops)  21.9 us
    ppermute x14, waiting for transfers between devices, down(): return lax.ppermute(value, 'tp', self.down_hops)  18.4 us
    ppermute x14, waiting for transfers between devices, up(): return lax.ppermute(value, 'tp', self.up_hops)  14.5 us
    ppermute x14, starting transfers between devices, down(): return lax.ppermute(value, 'tp', self.down_hops)  8.84 us
    ppermute x22, starting transfers between devices, swap_cores(): return lax.ppermute(value, 'dp', [(0, 1), (1, 0)])  5.34 us
  transfers between devices with their start and end apart: 50, of which 18 were waited for; matrix products, arithmetic and copies ran while one was open for 40% of the time, Pallas kernels for 0%

profile of v4, /device:TPU:0, one launch (start us, length us, event | category | flops | bytes accessed | tf_op | source)
XLA Modules:
  0.0 124.1 jit_solution(5481842328039489628)
XLA Ops:
  0.6 3.1 %collective-permute-start = (bf16[256,512]{1,0:T(8,128)(2,1)}, bf16[256,512]{1,0:T(8,128)(2,1)S(1)}, u32[]{:S(2)}, u32[]{:S(2)}) collective-permute-start(bf16[256,512]{1,0:T(8,128)(2,1)} %param.5), channel_id=1, source_target_pairs={{0,4},{4,8},{8,12},{12,14},{14,10},{10,6},{6,2},{2,0},{1,5},{5,9},... | collective-permute-start | bytes 786440 | tf_op jit(solution)/shard_map/ppermute | solution.py:25
  3.7 2.0 %collective-permute-start.6 = (bf16[256,512]{1,0:T(8,128)(2,1)}, bf16[256,512]{1,0:T(8,128)(2,1)S(1)}, u32[]{:S(2)}, u32[]{:S(2)}) collective-permute-start(bf16[256,512]{1,0:T(8,128)(2,1)} %param.9), channel_id=1, source_target_pairs={{0,4},{4,8},{8,12},{12,14},{14,10},{10,6},{6,2},{2,0},{1,5},{5,9},... | collective-permute-start | bytes 786440 | tf_op jit(solution)/shard_map/ppermute | solution.py:25
  5.7 5.3 %collective-permute-done = bf16[256,512]{1,0:T(8,128)(2,1)S(1)} collective-permute-done((bf16[256,512]{1,0:T(8,128)(2,1)}, bf16[256,512]{1,0:T(8,128)(2,1)S(1)}, u32[]{:S(2)}, u32[]{:S(2)}) %collective-permute-start) | collective-permute-done | bytes 262176 | tf_op jit(solution)/shard_map/ppermute | solution.py:25
  11.0 2.2 %collective-permute-done.1 = bf16[256,512]{1,0:T(8,128)(2,1)S(1)} collective-permute-done((bf16[256,512]{1,0:T(8,128)(2,1)}, bf16[256,512]{1,0:T(8,128)(2,1)S(1)}, u32[]{:S(2)}, u32[]{:S(2)}) %collective-permute-start.1) | collective-permute-done | bytes 262176 | tf_op jit(solution)/shard_map/ppermute | solution.py:28
  13.2 2.0 %collective-permute-start.3 = (bf16[256,512]{1,0:T(8,128)(2,1)S(1)}, bf16[256,512]{1,0:T(8,128)(2,1)S(1)}, u32[]{:S(2)}, u32[]{:S(2)}) collective-permute-start(bf16[256,512]{1,0:T(8,128)(2,1)S(1)} %collective-permute-done), channel_id=1, source_target_pairs={{0,4},{4,8},{8,12},{12,14},{14,10},{10,6},{6,2},{2,0},{1,5},{5,9},... | collective-permute-start | bytes 786440 | tf_op jit(solution)/shard_map/ppermute | solution.py:25
  16.6 2.2 %collective-permute-done.7 = bf16[256,512]{1,0:T(8,128)(2,1)S(1)} collective-permute-done((bf16[256,512]{1,0:T(8,128)(2,1)}, bf16[256,512]{1,0:T(8,128)(2,1)S(1)}, u32[]{:S(2)}, u32[]{:S(2)}) %collective-permute-start.7) | collective-permute-done | bytes 262176 | tf_op jit(solution)/shard_map/ppermute | solution.py:28
  18.8 2.0 %collective-permute-start.9 = (bf16[256,512]{1,0:T(8,128)(2,1)S(1)}, bf16[256,512]{1,0:T(8,128)(2,1)S(1)}, u32[]{:S(2)}, u32[]{:S(2)}) collective-permute-start(bf16[256,512]{1,0:T(8,128)(2,1)S(1)} %collective-permute-done.6), channel_id=1, source_target_pairs={{0,4},{4,8},{8,12},{12,14},{14,10},{10,6},{6,2},{2,0},{1,5},{5,9},... | collective-permute-start | bytes 786440 | tf_op jit(solution)/shard_map/ppermute | solution.py:25
  20.8 3.6 %collective-permute-done.2 = bf16[256,512]{1,0:T(8,128)(2,1)S(1)} collective-permute-done((bf16[256,512]{1,0:T(8,128)(2,1)S(1)}, bf16[256,512]{1,0:T(8,128)(2,1)S(1)}, u32[]{:S(2)}, u32[]{:S(2)}) %collective-permute-start.2) | collective-permute-done | bytes 262176 | tf_op jit(solution)/shard_map/ppermute | solution.py:28
  26.7 3.3 %collective-permute-done.8 = bf16[256,512]{1,0:T(8,128)(2,1)S(1)} collective-permute-done((bf16[256,512]{1,0:T(8,128)(2,1)S(1)}, bf16[256,512]{1,0:T(8,128)(2,1)S(1)}, u32[]{:S(2)}, u32[]{:S(2)}) %collective-permute-start.8) | collective-permute-done | bytes 262176 | tf_op jit(solution)/shard_map/ppermute | solution.py:28
  32.3 3.3 %collective-permute-done.5 = bf16[256,512]{1,0:T(8,128)(2,1)S(1)} collective-permute-done((bf16[256,512]{1,0:T(8,128)(2,1)S(1)}, bf16[256,512]{1,0:T(8,128)(2,1)S(1)}, u32[]{:S(2)}, u32[]{:S(2)}) %collective-permute-start.5) | collective-permute-done | bytes 262176 | tf_op jit(solution)/shard_map/ppermute | solution.py:28
  37.4 2.3 %collective-permute-done.12 = bf16[256,512]{1,0:T(8,128)(2,1)S(1)} collective-permute-done((bf16[256,512]{1,0:T(8,128)(2,1)S(1)}, bf16[256,512]{1,0:T(8,128)(2,1)S(1)}, u32[]{:S(2)}, u32[]{:S(2)}) %collective-permute-start.12) | collective-permute-done | bytes 262176 | tf_op jit(solution)/shard_map/ppermute | solution.py:28
  41.5 2.9 %collective-permute-done.10 = bf16[256,512]{1,0:T(8,128)(2,1)S(1)} collective-permute-done((bf16[256,512]{1,0:T(8,128)(2,1)S(1)}, bf16[256,512]{1,0:T(8,128)(2,1)S(1)}, u32[]{:S(2)}, u32[]{:S(2)}) %collective-permute-start.10) | collective-permute-done | bytes 262176 | tf_op jit(solution)/shard_map/ppermute | solution.py:25
  45.8 2.1 %fusion.80 = f32[256,1792]{1,0:T(8,128)S(1)} fusion(bf16[256,2048]{1,0:T(8,128)(2,1)S(1)} %get-tuple-element.153, bf16[2048,1792]{1,0:T(8,128)(2,1)S(1)} %copy-done.2), kind=kOutput, calls=%fused_computation.117 | convolution fusion | flops 1879048192 | bytes 10223616 | tf_op jit(solution)/shard_map/dot_general | solution.py:49
  48.8 2.1 %fusion.81 = f32[256,1792]{1,0:T(8,128)S(1)} fusion(bf16[256,2048]{1,0:T(8,128)(2,1)S(1)} %get-tuple-element.153, bf16[2048,1792]{1,0:T(8,128)(2,1)S(1)} %bitcast.30), kind=kOutput, calls=%fused_computation.118 | convolution fusion | flops 1879048192 | bytes 10223616 | tf_op jit(solution)/shard_map/dot_general | solution.py:49
  53.9 2.1 %convolution_convert_fusion.4 = bf16[256,1792]{1,0:T(8,128)(2,1)S(1)} fusion(bf16[256,2048]{1,0:T(8,128)(2,1)S(1)} %constant_dynamic-update-slice_fusion.10, bf16[2048,1792]{1,0:T(8,128)(2,1)S(1)} %bitcast.30), kind=kOutput, calls=%fused_computation.4 | convolution fusion | flops 1879506944 | bytes 9306112 | tf_op jit(solution)/shard_map/dot_general | solution.py:49
  56.0 2.1 %convolution_convert_fusion.5 = bf16[256,1792]{1,0:T(8,128)(2,1)S(1)} fusion(bf16[256,2048]{1,0:T(8,128)(2,1)S(1)} %constant_dynamic-update-slice_fusion.10, bf16[2048,1792]{1,0:T(8,128)(2,1)S(1)} %copy-done.2), kind=kOutput, calls=%fused_computation.5 | convolution fusion | flops 1879506944 | bytes 9306112 | tf_op jit(solution)/shard_map/dot_general | solution.py:49
  58.7 2.1 %convolution_convert_fusion.3 = bf16[256,1792]{1,0:T(8,128)(2,1)S(1)} fusion(bf16[256,2048]{1,0:T(8,128)(2,1)S(1)} %constant_dynamic-update-slice_fusion.6, bf16[1792,2048]{1,0:T(8,128)(2,1)S(1)} %bitcast.28), kind=kOutput, calls=%fused_computation.3 | convolution fusion | flops 1879506944 | bytes 9306112 | tf_op jit(solution)/shard_map/dot_general | solution.py:49
  61.0 2.1 %fusion.82 = f32[256,1792]{1,0:T(8,128)S(1)} fusion(bf16[256,2048]{1,0:T(8,128)(2,1)S(1)} %get-tuple-element.102, bf16[1792,2048]{1,0:T(8,128)(2,1)S(1)} %bitcast.28), kind=kOutput, calls=%fused_computation.119 | convolution fusion | flops 1879048192 | bytes 10223616 | tf_op jit(solution)/shard_map/dot_general | solution.py:49
  91.3 2.0 %collective-permute-done.37 = bf16[256,512]{1,0:T(8,128)(2,1)S(1)} collective-permute-done((bf16[256,512]{1,0:T(8,128)(2,1)S(1)}, bf16[256,512]{1,0:T(8,128)(2,1)S(1)}, u32[]{:S(2)}, u32[]{:S(2)}) %collective-permute-start.37) | collective-permute-done | bytes 262176 | tf_op jit(solution)/shard_map/ppermute | solution.py:25
  93.3 1.8 %collective-permute-start.40 = (bf16[256,512]{1,0:T(8,128)(2,1)S(1)}, bf16[256,512]{1,0:T(8,128)(2,1)S(1)}, u32[]{:S(2)}, u32[]{:S(2)}) collective-permute-start(bf16[256,512]{1,0:T(8,128)(2,1)S(1)} %get-tuple-element.124), channel_id=1, source_target_pairs={{4,0},{8,4},{12,8},{14,12},{10,14},{6,10},{2,6},{0,2},{5,1},{9,5},... | collective-permute-start | bytes 786440 | tf_op jit(solution)/shard_map/ppermute | solution.py:28
  95.4 6.0 %convolution_convert_fusion.2 = bf16[1792,2048]{1,0:T(8,128)(2,1)} fusion(bf16[512,1792]{1,0:T(8,128)(2,1)S(1)} %constant_dynamic-update-slice_fusion, bf16[256,2048]{1,0:T(8,128)(2,1)S(1)} %constant_dynamic-update-slice_fusion.6, bf16[256,2048]{1,0:T(8,128)(2,1)S(1)} %get-tuple-element.102), kind=kOutput, calls=%fused_computation.2 | convolution fusion | flops 3765960704 | bytes 11272192 | tf_op jit(solution)/shard_map/dot_general | solution.py:49
  105.9 6.1 %convolution_convert_fusion.1 = bf16[2048,1792]{1,0:T(8,128)(2,1)} fusion(bf16[512,1792]{1,0:T(8,128)(2,1)S(1)} %constant_dynamic-update-slice_fusion.2, bf16[256,2048]{1,0:T(8,128)(2,1)S(1)} %constant_dynamic-update-slice_fusion.10, bf16[256,2048]{1,0:T(8,128)(2,1)S(1)} %get-tuple-element.153), kind=kOutput, calls=%fused_computation.1 | convolution fusion | flops 3765960704 | bytes 11272192 | tf_op jit(solution)/shard_map/dot_general | solution.py:49
  114.3 2.1 %collective-permute-done.41 = bf16[256,512]{1,0:T(8,128)(2,1)S(1)} collective-permute-done((bf16[256,512]{1,0:T(8,128)(2,1)S(1)}, bf16[256,512]{1,0:T(8,128)(2,1)S(1)}, u32[]{:S(2)}, u32[]{:S(2)}) %collective-permute-start.41) | collective-permute-done | bytes 262176 | tf_op jit(solution)/shard_map/ppermute | solution.py:25
  116.4 6.1 %convolution_convert_fusion = bf16[2048,1792]{1,0:T(8,128)(2,1)} fusion(bf16[512,1792]{1,0:T(8,128)(2,1)S(1)} %constant_dynamic-update-slice_fusion.4, bf16[256,2048]{1,0:T(8,128)(2,1)S(1)} %constant_dynamic-update-slice_fusion.10, bf16[256,2048]{1,0:T(8,128)(2,1)S(1)} %get-tuple-element.153), kind=kOutput, calls=%fused_computation | convolution fusion | flops 3765960704 | bytes 11272192 | tf_op jit(solution)/shard_map/dot_general | solution.py:49
  (172 shorter events, 52.0 us)
Async XLA Ops:
  0.6 10.4 %collective-permute-start = (bf16[256,512]{1,0:T(8,128)(2,1)}, bf16[256,512]{1,0:T(8,128)(2,1)S(1)}, u32[]{:S(2)}, u32[]{:S(2)}) collective-permute-start(bf16[256,512]{1,0:T(8,128)(2,1)} %param.5), channel_id=1, source_target_pairs={{0,4},{4,8},{8,12},{12,14},{14,10},{10,6},{6,2},{2,0},{1,5},{5,9},... | collective-permute-start | bytes 786440 | tf_op jit(solution)/shard_map/ppermute | solution.py:25
  3.7 12.9 %collective-permute-start.6 = (bf16[256,512]{1,0:T(8,128)(2,1)}, bf16[256,512]{1,0:T(8,128)(2,1)S(1)}, u32[]{:S(2)}, u32[]{:S(2)}) collective-permute-start(bf16[256,512]{1,0:T(8,128)(2,1)} %param.9), channel_id=1, source_target_pairs={{0,4},{4,8},{8,12},{12,14},{14,10},{10,6},{6,2},{2,0},{1,5},{5,9},... | collective-permute-start | bytes 786440 | tf_op jit(solution)/shard_map/ppermute | solution.py:25
  5.7 13.0 %collective-permute-start.7 = (bf16[256,512]{1,0:T(8,128)(2,1)}, bf16[256,512]{1,0:T(8,128)(2,1)S(1)}, u32[]{:S(2)}, u32[]{:S(2)}) collective-permute-start(bf16[256,512]{1,0:T(8,128)(2,1)} %param.9), channel_id=1, source_target_pairs={{4,0},{8,4},{12,8},{14,12},{10,14},{6,10},{2,6},{0,2},{5,1},{9,5},... | collective-permute-start | bytes 786440 | tf_op jit(solution)/shard_map/ppermute | solution.py:28
  13.1 11.2 %collective-permute-start.2 = (bf16[256,512]{1,0:T(8,128)(2,1)S(1)}, bf16[256,512]{1,0:T(8,128)(2,1)S(1)}, u32[]{:S(2)}, u32[]{:S(2)}) collective-permute-start(bf16[256,512]{1,0:T(8,128)(2,1)S(1)} %collective-permute-done.1), channel_id=1, source_target_pairs={{4,0},{8,4},{12,8},{14,12},{10,14},{6,10},{2,6},{0,2},{5,1},{9,5},... | collective-permute-start | bytes 786440 | tf_op jit(solution)/shard_map/ppermute | solution.py:28
  13.2 11.2 %collective-permute-start.3 = (bf16[256,512]{1,0:T(8,128)(2,1)S(1)}, bf16[256,512]{1,0:T(8,128)(2,1)S(1)}, u32[]{:S(2)}, u32[]{:S(2)}) collective-permute-start(bf16[256,512]{1,0:T(8,128)(2,1)S(1)} %collective-permute-done), channel_id=1, source_target_pairs={{0,4},{4,8},{8,12},{12,14},{14,10},{10,6},{6,2},{2,0},{1,5},{5,9},... | collective-permute-start | bytes 786440 | tf_op jit(solution)/shard_map/ppermute | solution.py:25
  18.8 11.2 %collective-permute-start.8 = (bf16[256,512]{1,0:T(8,128)(2,1)S(1)}, bf16[256,512]{1,0:T(8,128)(2,1)S(1)}, u32[]{:S(2)}, u32[]{:S(2)}) collective-permute-start(bf16[256,512]{1,0:T(8,128)(2,1)S(1)} %collective-permute-done.7), channel_id=1, source_target_pairs={{4,0},{8,4},{12,8},{14,12},{10,14},{6,10},{2,6},{0,2},{5,1},{9,5},... | collective-permute-start | bytes 786440 | tf_op jit(solution)/shard_map/ppermute | solution.py:28
  18.8 11.2 %collective-permute-start.9 = (bf16[256,512]{1,0:T(8,128)(2,1)S(1)}, bf16[256,512]{1,0:T(8,128)(2,1)S(1)}, u32[]{:S(2)}, u32[]{:S(2)}) collective-permute-start(bf16[256,512]{1,0:T(8,128)(2,1)S(1)} %collective-permute-done.6), channel_id=1, source_target_pairs={{0,4},{4,8},{8,12},{12,14},{14,10},{10,6},{6,2},{2,0},{1,5},{5,9},... | collective-permute-start | bytes 786440 | tf_op jit(solution)/shard_map/ppermute | solution.py:25
  24.4 11.2 %collective-permute-start.4 = (bf16[256,512]{1,0:T(8,128)(2,1)S(1)}, bf16[256,512]{1,0:T(8,128)(2,1)S(1)}, u32[]{:S(2)}, u32[]{:S(2)}) collective-permute-start(bf16[256,512]{1,0:T(8,128)(2,1)S(1)} %collective-permute-done.3), channel_id=1, source_target_pairs={{0,4},{4,8},{8,12},{12,14},{14,10},{10,6},{6,2},{2,0},{1,5},{5,9},... | collective-permute-start | bytes 786440 | tf_op jit(solution)/shard_map/ppermute | solution.py:25
  26.0 9.7 %collective-permute-start.5 = (bf16[256,512]{1,0:T(8,128)(2,1)S(1)}, bf16[256,512]{1,0:T(8,128)(2,1)S(1)}, u32[]{:S(2)}, u32[]{:S(2)}) collective-permute-start(bf16[256,512]{1,0:T(8,128)(2,1)S(1)} %collective-permute-done.2), channel_id=1, source_target_pairs={{4,0},{8,4},{12,8},{14,12},{10,14},{6,10},{2,6},{0,2},{5,1},{9,5},... | collective-permute-start | bytes 786440 | tf_op jit(solution)/shard_map/ppermute | solution.py:28
  26.6 13.9 %collective-permute-start.13 = (bf16[256,512]{1,0:T(8,128)(2,1)S(1)}, bf16[256,512]{1,0:T(8,128)(2,1)S(1)}, u32[]{:S(2)}, u32[]{:S(2)}) collective-permute-start(bf16[256,512]{1,0:T(8,128)(2,1)S(1)} %get-tuple-element.158), channel_id=1, source_target_pairs={{0,1},{1,0},{2,3},{3,2},{4,5},{5,4},{6,7},{7,6},{8,9},{9,8},{10,11... | collective-permute-start | bytes 786440 | tf_op jit(solution)/shard_map/ppermute | solution.py:41
  30.0 9.8 %collective-permute-start.11 = (bf16[256,512]{1,0:T(8,128)(2,1)S(1)}, bf16[256,512]{1,0:T(8,128)(2,1)S(1)}, u32[]{:S(2)}, u32[]{:S(2)}) collective-permute-start(bf16[256,512]{1,0:T(8,128)(2,1)S(1)} %collective-permute-done.9), channel_id=1, source_target_pairs={{0,4},{4,8},{8,12},{12,14},{14,10},{10,6},{6,2},{2,0},{1,5},{5,9},... | collective-permute-start | bytes 786440 | tf_op jit(solution)/shard_map/ppermute | solution.py:25
  39.8 13.2 %collective-permute-start.15 = (bf16[256,512]{1,0:T(8,128)(2,1)S(1)}, bf16[256,512]{1,0:T(8,128)(2,1)S(1)}, u32[]{:S(2)}, u32[]{:S(2)}) collective-permute-start(bf16[256,512]{1,0:T(8,128)(2,1)S(1)} %get-tuple-element.154), channel_id=1, source_target_pairs={{0,1},{1,0},{2,3},{3,2},{4,5},{5,4},{6,7},{7,6},{8,9},{9,8},{10,11... | collective-permute-start | bytes 786440 | tf_op jit(solution)/shard_map/ppermute | solution.py:41
  39.8 12.6 %collective-permute-start.14 = (bf16[256,512]{1,0:T(8,128)(2,1)S(1)}, bf16[256,512]{1,0:T(8,128)(2,1)S(1)}, u32[]{:S(2)}, u32[]{:S(2)}) collective-permute-start(bf16[256,512]{1,0:T(8,128)(2,1)S(1)} %get-tuple-element.156), channel_id=1, source_target_pairs={{0,1},{1,0},{2,3},{3,2},{4,5},{5,4},{6,7},{7,6},{8,9},{9,8},{10,11... | collective-permute-start | bytes 786440 | tf_op jit(solution)/shard_map/ppermute | solution.py:41
  40.5 12.6 %collective-permute-start.24 = (bf16[256,512]{1,0:T(8,128)(2,1)S(1)}, bf16[256,512]{1,0:T(8,128)(2,1)S(1)}, u32[]{:S(2)}, u32[]{:S(2)}) collective-permute-start(bf16[256,512]{1,0:T(8,128)(2,1)S(1)} %get-tuple-element.147), channel_id=1, source_target_pairs={{0,1},{1,0},{2,3},{3,2},{4,5},{5,4},{6,7},{7,6},{8,9},{9,8},{10,11... | collective-permute-start | bytes 786440 | tf_op jit(solution)/shard_map/ppermute | solution.py:41
  40.8 12.3 %collective-permute-start.23 = (bf16[256,512]{1,0:T(8,128)(2,1)S(1)}, bf16[256,512]{1,0:T(8,128)(2,1)S(1)}, u32[]{:S(2)}, u32[]{:S(2)}) collective-permute-start(bf16[256,512]{1,0:T(8,128)(2,1)S(1)} %get-tuple-element.149), channel_id=1, source_target_pairs={{0,1},{1,0},{2,3},{3,2},{4,5},{5,4},{6,7},{7,6},{8,9},{9,8},{10,11... | collective-permute-start | bytes 786440 | tf_op jit(solution)/shard_map/ppermute | solution.py:41
  83.4 9.9 %collective-permute-start.38 = (bf16[256,512]{1,0:T(8,128)(2,1)S(1)}, bf16[256,512]{1,0:T(8,128)(2,1)S(1)}, u32[]{:S(2)}, u32[]{:S(2)}) collective-permute-start(bf16[256,512]{1,0:T(8,128)(2,1)S(1)} %broadcast_select_fusion.3), channel_id=1, source_target_pairs={{4,0},{8,4},{12,8},{14,12},{10,14},{6,10},{2,6},{0,2},{5,1},{9,5},... | collective-permute-start | bytes 786440 | tf_op jit(solution)/shard_map/ppermute | solution.py:28
  85.5 15.9 %collective-permute-start.45 = (bf16[256,512]{1,0:T(8,128)(2,1)S(1)}, bf16[256,512]{1,0:T(8,128)(2,1)S(1)}, u32[]{:S(2)}, u32[]{:S(2)}) collective-permute-start(bf16[256,512]{1,0:T(8,128)(2,1)S(1)} %select_add_fusion.7), channel_id=1, source_target_pairs={{4,0},{8,4},{12,8},{14,12},{10,14},{6,10},{2,6},{0,2},{5,1},{9,5},... | collective-permute-start | bytes 786440 | tf_op jit(solution)/shard_map/ppermute | solution.py:28
  87.5 13.9 %collective-permute-start.44 = (bf16[256,512]{1,0:T(8,128)(2,1)S(1)}, bf16[256,512]{1,0:T(8,128)(2,1)S(1)}, u32[]{:S(2)}, u32[]{:S(2)}) collective-permute-start(bf16[256,512]{1,0:T(8,128)(2,1)S(1)} %broadcast_select_fusion), channel_id=1, source_target_pairs={{0,4},{4,8},{8,12},{12,14},{14,10},{10,6},{6,2},{2,0},{1,5},{5,9},... | collective-permute-start | bytes 786440 | tf_op jit(solution)/shard_map/ppermute | solution.py:25
  93.3 10.4 %collective-permute-start.40 = (bf16[256,512]{1,0:T(8,128)(2,1)S(1)}, bf16[256,512]{1,0:T(8,128)(2,1)S(1)}, u32[]{:S(2)}, u32[]{:S(2)}) collective-permute-start(bf16[256,512]{1,0:T(8,128)(2,1)S(1)} %get-tuple-element.124), channel_id=1, source_target_pairs={{4,0},{8,4},{12,8},{14,12},{10,14},{6,10},{2,6},{0,2},{5,1},{9,5},... | collective-permute-start | bytes 786440 | tf_op jit(solution)/shard_map/ppermute | solution.py:28
  101.5 10.4 %collective-permute-start.46 = (bf16[256,512]{1,0:T(8,128)(2,1)S(1)}, bf16[256,512]{1,0:T(8,128)(2,1)S(1)}, u32[]{:S(2)}, u32[]{:S(2)}) collective-permute-start(bf16[256,512]{1,0:T(8,128)(2,1)S(1)} %get-tuple-element.129), channel_id=1, source_target_pairs={{0,4},{4,8},{8,12},{12,14},{14,10},{10,6},{6,2},{2,0},{1,5},{5,9},... | collective-permute-start | bytes 786440 | tf_op jit(solution)/shard_map/ppermute | solution.py:25
  103.8 18.6 %collective-permute-start.42 = (bf16[256,512]{1,0:T(8,128)(2,1)S(1)}, bf16[256,512]{1,0:T(8,128)(2,1)S(1)}, u32[]{:S(2)}, u32[]{:S(2)}) collective-permute-start(bf16[256,512]{1,0:T(8,128)(2,1)S(1)} %select_add_fusion.4), channel_id=1, source_target_pairs={{4,0},{8,4},{12,8},{14,12},{10,14},{6,10},{2,6},{0,2},{5,1},{9,5},... | collective-permute-start | bytes 786440 | tf_op jit(solution)/shard_map/ppermute | solution.py:28
  105.6 10.8 %collective-permute-start.41 = (bf16[256,512]{1,0:T(8,128)(2,1)S(1)}, bf16[256,512]{1,0:T(8,128)(2,1)S(1)}, u32[]{:S(2)}, u32[]{:S(2)}) collective-permute-start(bf16[256,512]{1,0:T(8,128)(2,1)S(1)} %select_add_fusion.9), channel_id=1, source_target_pairs={{0,4},{4,8},{8,12},{12,14},{14,10},{10,6},{6,2},{2,0},{1,5},{5,9},... | collective-permute-start | bytes 786440 | tf_op jit(solution)/shard_map/ppermute | solution.py:25
  112.2 11.1 %collective-permute-start.48 = (bf16[256,512]{1,0:T(8,128)(2,1)S(1)}, bf16[256,512]{1,0:T(8,128)(2,1)S(1)}, u32[]{:S(2)}, u32[]{:S(2)}) collective-permute-start(bf16[256,512]{1,0:T(8,128)(2,1)S(1)} %select_add_fusion.3), channel_id=1, source_target_pairs={{0,4},{4,8},{8,12},{12,14},{14,10},{10,6},{6,2},{2,0},{1,5},{5,9},... | collective-permute-start | bytes 786440 | tf_op jit(solution)/shard_map/ppermute | solution.py:25
  113.8 9.5 %collective-permute-start.49 = (bf16[256,512]{1,0:T(8,128)(2,1)S(1)}, bf16[256,512]{1,0:T(8,128)(2,1)S(1)}, u32[]{:S(2)}, u32[]{:S(2)}) collective-permute-start(bf16[256,512]{1,0:T(8,128)(2,1)S(1)} %select_add_fusion), channel_id=1, source_target_pairs={{4,0},{8,4},{12,8},{14,12},{10,14},{6,10},{2,6},{0,2},{5,1},{9,5},... | collective-permute-start | bytes 786440 | tf_op jit(solution)/shard_map/ppermute | solution.py:28
  (37 other events, 204.1 us)
